TPU v7x, 128 devices: a whole 4x4x4 slice. The times are simulated.
128 devices in a mesh: dp: 16 (over x, z), tensor: 8 (over y, core).
Axes of the slice: x: 4, y: 4, z: 4, core: 2. Of those that a mesh axis runs over, the one named last changes fastest.
Arguments:
- tokens: bfloat16 [16384, 2560], P(('dp', 'tensor')), may hold values from -6 to 6
- out_grad: bfloat16 [16384, 2560], P(('dp', 'tensor')), may hold values from -0.75 to 0.75
- routing: int32 [16384, 1], P(('dp', 'tensor')), may hold values from 0 to 15; in each aligned block of 128 rows (0 to 127, 128 to 255, ...) at most 12 rows name the same one
- router_weight: bfloat16 [2560, 16], replicated, may hold values from -0.125 to 0.125
- gate_weight: bfloat16 [16, 2560, 4096], P('dp', None, 'tensor'), may hold values from -0.125 to 0.125
- up_weight: bfloat16 [16, 2560, 4096], P('dp', None, 'tensor'), may hold values from -0.125 to 0.125
- down_weight: bfloat16 [16, 4096, 2560], P('dp', 'tensor'), may hold values from -0.09375 to 0.09375
- saved_gate: bfloat16 [16, 1536, 4096], P('dp', None, 'tensor'), may hold values from -6 to 6
- saved_up: bfloat16 [16, 1536, 4096], P('dp', None, 'tensor'), may hold values from -6 to 6
Outputs:
- grad_tokens: bfloat16 [16384, 2560], P(('dp', 'tensor'))
- grad_gate: bfloat16 [16, 2560, 4096], P('dp', None, 'tensor')
- grad_up: bfloat16 [16, 2560, 4096], P('dp', None, 'tensor')
- grad_down: bfloat16 [16, 4096, 2560], P('dp', 'tensor')
- grad_router: float32 [2560, 16], replicated
Inputs may be any that keep to these rules, and one draw needn't show every extreme that they name: `routing`: within the 128 rows of one device no expert is named by more than 12 rows; in every draw some device's rows name some expert exactly 12 times.
All inputs are finite; a program needn't handle non-finite values.
Results may differ from a plain program's by a relative error of at most 0.015.
Values may be sent and summed in bfloat16 or wider, within the bound.
A program may use at most 192 MiB of HBM per device.

v0:
```python
import jax
import jax.numpy as jnp
from jax import lax
from jax.sharding import PartitionSpec as P


def local(
    tokens,
    out_grad,
    routing,
    router_weight,
    gate_weight,
    up_weight,
    down_weight,
    saved_gate,
    saved_up,
):
    rows_count = lax.axis_size("dp")
    group_count = lax.axis_size("tensor")
    features = tokens.shape[1]
    experts = router_weight.shape[1]
    slot_total = saved_gate.shape[1]
    capacity = slot_total // (rows_count * group_count)
    chosen = routing[:, 0]
    onehot = (chosen[:, None] == jnp.arange(experts, dtype=jnp.int32)[None, :]).astype(jnp.int32)
    earlier = jnp.cumsum(onehot, axis=0) - onehot
    slot_index = jnp.sum(earlier * onehot, axis=1)
    target_row = chosen * capacity + slot_index
    placing = (
        jnp.arange(experts * capacity, dtype=jnp.int32)[:, None] == target_row[None, :]
    ).astype(jnp.bfloat16)
    onehot_float = onehot.astype(jnp.float32)
    logits = jnp.dot(tokens, router_weight, preferred_element_type=jnp.float32)
    gate_score = jax.nn.sigmoid(jnp.sum(logits * onehot_float, axis=1))
    scaled = (gate_score[:, None] * tokens.astype(jnp.float32)).astype(jnp.bfloat16)
    send_in = jnp.dot(placing, scaled, preferred_element_type=jnp.float32).astype(jnp.bfloat16)
    send_in = send_in.reshape(experts, capacity, features)
    send_grad = jnp.dot(placing, out_grad, preferred_element_type=jnp.float32).astype(jnp.bfloat16)
    send_grad = send_grad.reshape(experts, capacity, features)
    spread_in = jnp.broadcast_to(send_in[:, None], (experts, group_count, capacity, features))
    spread_grad = jnp.broadcast_to(send_grad[:, None], (experts, group_count, capacity, features))
    spread_in = spread_in.reshape(experts * group_count, capacity, features)
    spread_grad = spread_grad.reshape(experts * group_count, capacity, features)
    got_in, got_grad = (
        lax.all_to_all(spread_in, ("dp", "tensor"), split_axis=0, concat_axis=0, tiled=True),
        lax.all_to_all(spread_grad, ("dp", "tensor"), split_axis=0, concat_axis=0, tiled=True),
    )
    expert_in = got_in.reshape(slot_total, features)
    expert_grad = got_grad.reshape(slot_total, features)
    gate_f = saved_gate[0].astype(jnp.float32)
    up_f = saved_up[0].astype(jnp.float32)
    sigmoid_a = jax.nn.sigmoid(gate_f)
    silu_a = gate_f * sigmoid_a
    hidden = (silu_a * up_f).astype(jnp.bfloat16)
    grad_hidden = lax.dot_general(
        expert_grad, down_weight[0], (((1,), (1,)), ((), ())), preferred_element_type=jnp.float32
    )
    grad_a = (grad_hidden * up_f * sigmoid_a * (1.0 + gate_f * (1.0 - sigmoid_a))).astype(
        jnp.bfloat16
    )
    grad_b = (grad_hidden * silu_a).astype(jnp.bfloat16)
    rows_dims = (((0,), (0,)), ((), ()))
    grad_down = lax.dot_general(hidden, expert_grad, rows_dims, preferred_element_type=jnp.float32)
    grad_gate = lax.dot_general(expert_in, grad_a, rows_dims, preferred_element_type=jnp.float32)
    grad_up = lax.dot_general(expert_in, grad_b, rows_dims, preferred_element_type=jnp.float32)
    hidden_dims = (((1,), (1,)), ((), ()))
    partial_value = lax.dot_general(
        grad_a, gate_weight[0], hidden_dims, preferred_element_type=jnp.float32
    )
    partial_value = partial_value + lax.dot_general(
        grad_b, up_weight[0], hidden_dims, preferred_element_type=jnp.float32
    )
    partial_rounded = partial_value.astype(jnp.bfloat16)
    pieces = partial_rounded.reshape(rows_count * group_count, capacity, features)
    returned_parts = lax.all_to_all(
        pieces, ("dp", "tensor"), split_axis=0, concat_axis=0, tiled=True
    )
    summed = jnp.sum(
        returned_parts.reshape(experts, group_count, capacity, features).astype(jnp.float32), axis=1
    )
    returned = summed.astype(jnp.bfloat16)
    grad_scaled = lax.dot_general(
        placing,
        returned.reshape(experts * capacity, features),
        rows_dims,
        preferred_element_type=jnp.float32,
    )
    grad_score = jnp.sum(tokens.astype(jnp.float32) * grad_scaled, axis=1)
    grad_logit = grad_score * gate_score * (1.0 - gate_score)
    picked = lax.dot_general(
        onehot.astype(jnp.bfloat16), router_weight, hidden_dims, preferred_element_type=jnp.float32
    )
    grad_tokens = (gate_score[:, None] * grad_scaled + grad_logit[:, None] * picked).astype(
        jnp.bfloat16
    )
    router_part = jnp.dot(
        tokens.astype(jnp.float32).T,
        grad_logit[:, None] * onehot_float,
        precision=lax.Precision.HIGHEST,
    )
    grad_router = lax.psum(router_part, ("dp", "tensor"))
    return (
        grad_tokens,
        grad_gate.astype(jnp.bfloat16)[None],
        grad_up.astype(jnp.bfloat16)[None],
        grad_down.astype(jnp.bfloat16)[None],
        grad_router,
    )


def solution(mesh):
    placed = (
        P(("dp", "tensor"), None),
        P(("dp", "tensor"), None),
        P(("dp", "tensor"), None),
        P(),
        P("dp", None, "tensor"),
        P("dp", None, "tensor"),
        P("dp", "tensor", None),
        P("dp", None, "tensor"),
        P("dp", None, "tensor"),
    )
    return jax.shard_map(
        local,
        mesh=mesh,
        in_specs=placed,
        out_specs=(
            P(("dp", "tensor"), None),
            P("dp", None, "tensor"),
            P("dp", None, "tensor"),
            P("dp", "tensor", None),
            P(),
        ),
        check_vma=False,
    )
```

profile of v0, /device:TPU:1, one launch (start us, length us, event | category | flops | bytes accessed | tf_op | source)
XLA Modules:
  0.0 640.1 jit_solution(5719443356671686439)
XLA Ops:
  7.2 0.0 copy-start
  7.2 0.8 fusion.42
  8.0 0.1 copy.16
  8.1 0.2 reduce_window_sum.11
  8.3 0.1 copy.17
  8.3 0.7 fusion.40
  9.0 0.7 multiply_add_fusion
  9.7 2.4 convolution_convert_fusion.4
  12.1 2.2 broadcast_in_dim.14
  14.3 6.5 %broadcast_in_dim.15 = bf16[16,8,12,2560]{3,2,1,0:T(8,128)(2,1)} broadcast(bf16[16,12,2560]{2,1,0:T(8,128)(2,1)} %broadcast_in_dim.14), dimensions={0,2,3} | broadcast | bytes 8847360 | tf_op jit(solution)/shard_map/broadcast_in_dim | solution.py:41
  20.8 132.8 %all_to_all.15 = bf16[128,12,2560]{2,1,0:T(8,128)(2,1)} all-to-all(bf16[128,12,2560]{2,1,0:T(8,128)(2,1)} %bitcast.79), channel_id=1, replica_groups=mesh['dp'=16,'tensor'=8] {'dp','tensor'}, dimensions={0} | all-to-all | bytes 15728640 | tf_op jit(solution)/shard_map/all_to_all | solution.py:46
  153.6 12.8 %reshape.60 = bf16[1536,2560]{1,0:T(8,128)(2,1)} reshape(bf16[128,12,2560]{2,1,0:T(8,128)(2,1)} %all_to_all.15) | data formatting | bytes 15728640 | tf_op jit(solution)/shard_map/reshape | solution.py:49
  166.3 11.9 %fusion.11 = (bf16[1536,512]{1,0:T(8,128)(2,1)S(1)}, f32[1536,512]{1,0:T(8,128)}) fusion(bf16[1,1536,512]{2,1,0:T(8,128)(2,1)} %param.17, bf16[1,1536,512]{2,1,0:T(8,128)(2,1)} %param.16, bf16[1536,2560]{1,0:T(8,128)(2,1)} %reshape.60, bf16[1,512,2560]{2,1,0:T(8,128)(2,1)} %param.15), kind=kOutput, calls=%fused_computation.25 | convolution fusion | flops 4035969024 | bytes 18350080 | tf_op jit(solution)/shard_map/dot_general | solution.py:55
  178.2 0.0 copy-start.7
  178.2 0.0 copy-done
  178.2 7.8 %fusion.23 = f32[1536,2560]{1,0:T(8,128)} fusion(bf16[1536,512]{1,0:T(8,128)(2,1)S(1)} %get-tuple-element.7, bf16[1,2560,512]{2,1,0:T(8,128)(2,1)S(1)} %copy-done), kind=kOutput, calls=%fused_computation.37 | convolution fusion | flops 4026531840 | bytes 19922944 | tf_op jit(solution)/shard_map/dot_general | solution.py:67
  186.0 0.0 copy-done.7
  186.0 15.3 %add_convert_fusion = bf16[1536,2560]{1,0:T(8,128)(2,1)} fusion(f32[1536,2560]{1,0:T(8,128)} %fusion.23, bf16[1,2560,512]{2,1,0:T(8,128)(2,1)} %param.14, f32[1536,512]{1,0:T(8,128)} %get-tuple-element.8, bf16[1,1536,512]{2,1,0:T(8,128)(2,1)} %param.16), kind=kOutput, calls=%fused_computation | convolution fusion | flops 4039901184 | bytes 30932992 | tf_op jit(solution)/shard_map/dot_general | solution.py:70
  201.3 12.7 %reshape.61 = bf16[128,12,2560]{2,1,0:T(8,128)(2,1)} reshape(bf16[1536,2560]{1,0:T(8,128)(2,1)} %add_convert_fusion) | data formatting | bytes 15728640 | tf_op jit(solution)/shard_map/reshape | solution.py:74
  214.0 0.0 copy-start.2
  214.0 0.0 copy-start.4
  214.0 0.0 copy-start.5
  214.0 10.0 %all-to-all-start.1 = ((bf16[128,12,2560]{2,1,0:T(8,128)(2,1)}), bf16[128,12,2560]{2,1,0:T(8,128)(2,1)}, u32[]{:S(2)}, u32[]{:S(2)}) async-start(bf16[128,12,2560]{2,1,0:T(8,128)(2,1)} %reshape.61), calls=%async_computation.1 | async-start | bytes 20971520 | tf_op jit(solution)/shard_map/all_to_all | solution.py:75
  224.0 0.0 copy-done.2
  224.0 0.0 copy-done.4
  224.0 0.0 copy-done.5
  224.1 0.3 fusion.31
  224.3 132.2 %all-to-all-done.1 = bf16[128,12,2560]{2,1,0:T(8,128)(2,1)} async-done(((bf16[128,12,2560]{2,1,0:T(8,128)(2,1)}), bf16[128,12,2560]{2,1,0:T(8,128)(2,1)}, u32[]{:S(2)}, u32[]{:S(2)}) %all-to-all-start.1) | async-done | bytes 7864352 | tf_op jit(solution)/shard_map/all_to_all | solution.py:75
  356.5 5.9 bitcast_reduce_fusion
  362.4 1.1 reshape.63
  363.5 1.7 fusion.29
  365.2 1.5 convolution_convert_fusion.3
  366.6 2.2 broadcast_in_dim.32
  368.8 6.5 %broadcast_in_dim.33 = bf16[16,8,12,2560]{3,2,1,0:T(8,128)(2,1)} broadcast(bf16[16,12,2560]{2,1,0:T(8,128)(2,1)} %broadcast_in_dim.32), dimensions={0,2,3} | broadcast | bytes 8847360 | tf_op jit(solution)/shard_map/broadcast_in_dim | solution.py:40
  375.3 8.8 %all-to-all-start.2 = ((bf16[128,12,2560]{2,1,0:T(8,128)(2,1)}), bf16[128,12,2560]{2,1,0:T(8,128)(2,1)}, u32[]{:S(2)}, u32[]{:S(2)}) async-start(bf16[128,12,2560]{2,1,0:T(8,128)(2,1)} %bitcast.78), calls=%async_computation.2 | async-start | bytes 20971520 | tf_op jit(solution)/shard_map/all_to_all | solution.py:45
  384.1 0.0 all-reduce.2.cloned.1.call-start
  384.1 10.3 %fusion.5 = bf16[1,512,2560]{2,1,0:T(8,128)(2,1)} fusion(bf16[1536,2560]{1,0:T(8,128)(2,1)} %reshape.60, bf16[1,1536,512]{2,1,0:T(8,128)(2,1)} %param.17, bf16[1,1536,512]{2,1,0:T(8,128)(2,1)} %param.16), kind=kOutput, calls=%fused_computation.13 | convolution fusion | flops 4034134016 | bytes 13631488 | tf_op jit(solution)/shard_map/dot_general | solution.py:63
  394.4 1.0 convolution_bitcast_fusion
  395.4 0.0 all-reduce.2.cloned.1.call-update
  395.4 1.2 fusion.7
  396.6 0.0 copy-start.6
  396.6 121.9 %all-to-all-done.2 = bf16[128,12,2560]{2,1,0:T(8,128)(2,1)} async-done(((bf16[128,12,2560]{2,1,0:T(8,128)(2,1)}), bf16[128,12,2560]{2,1,0:T(8,128)(2,1)}, u32[]{:S(2)}, u32[]{:S(2)}) %all-to-all-start.2) | async-done | bytes 7864352 | tf_op jit(solution)/shard_map/all_to_all | solution.py:45
  518.5 12.8 %reshape.65 = bf16[1536,2560]{1,0:T(8,128)(2,1)} reshape(bf16[128,12,2560]{2,1,0:T(8,128)(2,1)} %all-to-all-done.2) | data formatting | bytes 15728640 | tf_op jit(solution)/shard_map/reshape | solution.py:48
  531.3 0.0 copy-done.6
  531.3 0.0 copy-start.3
  531.3 0.0 copy-start.8
  531.3 10.2 %fusion.4 = bf16[1,2560,512]{2,1,0:T(8,128)(2,1)} fusion(bf16[1536,2560]{1,0:T(8,128)(2,1)} %reshape.65, f32[1536,512]{1,0:T(8,128)} %get-tuple-element.8, bf16[1,1536,512]{2,1,0:T(8,128)(2,1)S(1)} %copy-done.6), kind=kOutput, calls=%fused_computation.12 | convolution fusion | flops 4033347584 | bytes 15204352 | tf_op jit(solution)/shard_map/dot_general | solution.py:65
  541.5 0.0 copy-done.3
  541.5 0.0 copy-done.8
  541.5 0.0 copy-start.1
  541.5 5.6 fusion.3
  547.1 84.6 %all-reduce.2.cloned.1.call-done = f32[2560,16]{0,1:T(8,128)} async-done(((f32[2560,16]{0,1:T(8,128)}), f32[2560,16]{0,1:T(8,128)}) %all-reduce.2.cloned.1.call-update) | async-done | bytes 163856 | tf_op jit(solution)/shard_map/psum | solution.py:101
  631.7 1.6 copy.19
  633.3 0.0 copy-done.1
  (1 shorter events, 0.0 us)
Async XLA Ops:
  7.2 171.1 %copy-start = (bf16[1,2560,512]{2,1,0:T(8,128)(2,1)S(1)}, bf16[1,2560,512]{2,1,0:T(8,128)(2,1)}, u32[]{:S(2)}) copy-start(bf16[1,2560,512]{2,1,0:T(8,128)(2,1)} %param.13) | copy-start | bytes 7864324
  178.2 7.8 %copy-start.7 = (bf16[1536,512]{1,0:T(8,128)(2,1)}, bf16[1536,512]{1,0:T(8,128)(2,1)S(1)}, u32[]{:S(2)}) copy-start(bf16[1536,512]{1,0:T(8,128)(2,1)S(1)} %get-tuple-element.7) | copy-start | bytes 4718596
  214.0 10.1 %copy-start.2 = (bf16[128,2560]{1,0:T(8,128)(2,1)S(1)}, bf16[128,2560]{1,0:T(8,128)(2,1)}, u32[]{:S(2)}) copy-start(bf16[128,2560]{1,0:T(8,128)(2,1)} %param.9) | copy-start | bytes 1966084
  214.0 10.1 %copy-start.4 = (bf16[2560,16]{0,1:T(8,128)(2,1)S(1)}, bf16[2560,16]{0,1:T(8,128)(2,1)}, u32[]{:S(2)}) copy-start(bf16[2560,16]{0,1:T(8,128)(2,1)} %param.12) | copy-start | bytes 245764
  214.0 10.1 %copy-start.5 = (s32[128,1]{0,1:T(1,128)S(1)}, s32[128,1]{0,1:T(1,128)}, u32[]{:S(2)}) copy-start(s32[128,1]{0,1:T(1,128)} %param.11) | copy-start | bytes 1540
  214.0 142.6 %all-to-all-start.1 = ((bf16[128,12,2560]{2,1,0:T(8,128)(2,1)}), bf16[128,12,2560]{2,1,0:T(8,128)(2,1)}, u32[]{:S(2)}, u32[]{:S(2)}) async-start(bf16[128,12,2560]{2,1,0:T(8,128)(2,1)} %reshape.61), calls=%async_computation.1 | async-start | bytes 20971520 | tf_op jit(solution)/shard_map/all_to_all | solution.py:75
  375.3 143.2 %all-to-all-start.2 = ((bf16[128,12,2560]{2,1,0:T(8,128)(2,1)}), bf16[128,12,2560]{2,1,0:T(8,128)(2,1)}, u32[]{:S(2)}, u32[]{:S(2)}) async-start(bf16[128,12,2560]{2,1,0:T(8,128)(2,1)} %bitcast.78), calls=%async_computation.2 | async-start | bytes 20971520 | tf_op jit(solution)/shard_map/all_to_all | solution.py:45
  384.1 247.6 %all-reduce.2.cloned.1.call-start = ((), (), s32[]{:S(2)}) async-start(), calls=%async_computation.3 | async-start | bytes 327680 | tf_op jit(solution)/shard_map/psum | solution.py:101
  396.6 134.6 %copy-start.6 = (bf16[1,1536,512]{2,1,0:T(8,128)(2,1)S(1)}, bf16[1,1536,512]{2,1,0:T(8,128)(2,1)}, u32[]{:S(2)}) copy-start(bf16[1,1536,512]{2,1,0:T(8,128)(2,1)} %param.16) | copy-start | bytes 4718596
  531.3 10.2 %copy-start.3 = (bf16[1536,2560]{1,0:T(8,128)(2,1)S(1)}, bf16[1536,2560]{1,0:T(8,128)(2,1)}, u32[]{:S(2)}) copy-start(bf16[1536,2560]{1,0:T(8,128)(2,1)} %reshape.65) | copy-start | bytes 23592964
  531.3 10.2 %copy-start.8 = (bf16[1536,512]{1,0:T(8,128)(2,1)S(1)}, bf16[1536,512]{1,0:T(8,128)(2,1)}, u32[]{:S(2)}) copy-start(bf16[1536,512]{1,0:T(8,128)(2,1)} %copy-done.7) | copy-start | bytes 4718596
  541.5 91.8 %copy-start.1 = (bf16[1,2560,512]{2,1,0:T(8,128)(2,1)S(1)}, bf16[1,2560,512]{2,1,0:T(8,128)(2,1)}, u32[]{:S(2)}) copy-start(bf16[1,2560,512]{2,1,0:T(8,128)(2,1)} %param.13) | copy-start | bytes 7864324
Sparse Core Ops, SparseCore 0:
  395.6 236.0 all-reduce.1
where the time goes:
time: 642 us; the launch traced here: 640 us
  waiting for transfers between devices  339 us (53%)
  blocking collectives  133 us (21%)
  matrix products  69.1 us (11%)
  local copies, waits for them, and re-layouts  58.3 us (9%)
  starting transfers between devices  18.9 us (3%)
  between operations  14.1 us (2%)
  other arithmetic  8.21 us (1%)
    all_to_all x1, blocking collectives, local(): lax.all_to_all(spread_grad, ('dp', 'tensor'), split_axis=0, concat_axis=0...  133 us
    all_to_all x1, waiting for transfers between devices, local(): lax.all_to_all(pieces, ('dp', 'tensor'), split_axis=0, concat_axis=0, til...  132 us
    all_to_all x1, waiting for transfers between devices, local(): lax.all_to_all(spread_in, ('dp', 'tensor'), split_axis=0, concat_axis=0,...  122 us
    psum x1, waiting for transfers between devices, local(): grad_router = lax.psum(router_part, ('dp', 'tensor'))  84.6 us
    dot_general x1, matrix products, local(): lax.dot_general(grad_b, up_weight[0], hidden_dims, preferred_element_type...  15.3 us
  transfers between devices with their start and end apart: 3, of which 3 were waited for; matrix products, arithmetic and copies ran while one was open for 6% of the time, Pallas kernels for 0%

commit v1 on v0

v1 whole, which is shorter than its diff:
```python
import jax
import jax.numpy as jnp
from jax import lax
from jax.experimental import pallas as pl
from jax.experimental.pallas import tpu as pltpu
from jax.sharding import PartitionSpec as P

MESH = pl.DeviceIdType.MESH
NN = (((1,), (0,)), ((), ()))
NT = (((1,), (1,)), ((), ()))
F32 = jnp.float32
BF16 = jnp.bfloat16

CHUNKS = 3
GROUPS = 4


def mm(a, b, dims=NN):
    return lax.dot_general(a, b, dims, preferred_element_type=F32)


def iota(shape, dim):
    return lax.broadcasted_iota(jnp.int32, shape, dim)


def eye_mask(n):
    return iota((n, n), 0) == iota((n, n), 1)


def kernel(
    routing_ref,
    tokens_hbm,
    out_grad_hbm,
    router_hbm,
    gate_hbm,
    up_hbm,
    down_hbm,
    saved_gate_hbm,
    saved_up_hbm,
    grad_tokens_hbm,
    grad_gate_hbm,
    grad_up_hbm,
    grad_down_hbm,
    grad_router_ref,
    tok,
    ogr,
    scaled,
    rw,
    gate,
    up,
    down,
    a_perm,
    b_perm,
    hid_t,
    ga,
    gb,
    send_g,
    send_i,
    recv_g,
    recv_i,
    recv_r,
    full_g,
    full_i,
    send_c,
    own_p,
    recv_c,
    st1_s,
    st1_r,
    st2_s,
    st2_r,
    unfold_m,
    fold_m,
    save_m,
    eye_m,
    gs,
    tgt_row,
    cols,
    rp_s,
    rp_r,
    rd_s,
    rd_r,
    ro_s,
    ro_r,
    load_sem,
    a2a_s,
    a2a_r,
    ag_s,
    ag_r,
    pc_s,
    pc_r,
    rs_s,
    rs_r,
    rt_s,
    rt_r,
    out_sem,
):
    d = lax.axis_index("dp")
    t = lax.axis_index("tensor")
    y = t // 2
    c = lax.rem(t, 2)
    right = (d, lax.rem(y + 1, 4) * 2 + c)
    left = (d, lax.rem(y + 3, 4) * 2 + c)
    partner = (d, y * 2 + 1 - c)
    mine = c * 4 + y
    from_left = c * 4 + lax.rem(y + 3, 4)
    from_right = c * 4 + lax.rem(y + 1, 4)
    far = c * 4 + lax.rem(y + 2, 4)
    dgw = tok.shape[1] // GROUPS
    rows = full_g.shape[1] * full_g.shape[2]
    width = tok.shape[1]

    loads = [
        pltpu.make_async_copy(src, dst, load_sem.at[n])
        for n, (src, dst) in enumerate(
            (
                (out_grad_hbm, ogr),
                (tokens_hbm, tok),
                (router_hbm, rw),
                (saved_gate_hbm, ga),
                (saved_up_hbm, gb),
                (down_hbm, down),
                (gate_hbm, gate),
                (up_hbm, up),
            )
        )
    ]
    for load in loads:
        load.start()

    barrier = pltpu.get_barrier_semaphore()

    @pl.loop(1, 16)
    def _(k):
        pl.semaphore_signal(
            barrier, inc=1, device_id=(lax.rem(d + k, 16), t), device_id_type=MESH
        )

    @pl.loop(1, 8)
    def _(k):
        pl.semaphore_signal(
            barrier, inc=1, device_id=(d, lax.rem(t + k, 8)), device_id_type=MESH
        )

    def remote(src, dst, send_sem, recv_sem, to):
        return pltpu.make_async_remote_copy(
            src_ref=src,
            dst_ref=dst,
            send_sem=send_sem,
            recv_sem=recv_sem,
            device_id=to,
            device_id_type=MESH,
        )

    def a2a_start(src, dst, kind, j):
        @pl.loop(1, 16)
        def _(k):
            to = lax.rem(d + k, 16)
            remote(
                src.at[j, to], dst.at[j, d], a2a_s.at[kind, j], a2a_r.at[kind, j], (to, t)
            ).start()

        dst[j, d] = src[j, d]

    def a2a_wait(dst, kind, j):
        part = dst.at[j, pl.ds(0, 15)]
        pltpu.make_async_copy(part, part, a2a_r.at[kind, j]).wait()

    def a2a_drain(src, kind, j):
        part = src.at[j, pl.ds(0, 15)]
        pltpu.make_async_copy(part, part, a2a_s.at[kind, j]).wait()

    def gather_copy(buf, kind, j, n):
        block, to = (
            (buf.at[j, mine], right),
            (buf.at[j, mine], left),
            (buf.at[j, from_left, pl.ds(0, 32)], right),
            (buf.at[j, from_right, pl.ds(32, 32)], left),
            (buf.at[j, mine], partner),
            (buf.at[j, from_left], partner),
            (buf.at[j, from_right], partner),
            (buf.at[j, far], partner),
        )[n]
        return remote(block, block, ag_s.at[kind, j, n], ag_r.at[kind, j, n], to)

    def gather_own(buf, kind, j):
        for n in (0, 1, 4):
            gather_copy(buf, kind, j, n).start()

    def landed(buf, kind, j, n):
        other = (1 - c) * 4
        block = (
            lambda: buf.at[j, from_left],
            lambda: buf.at[j, from_right],
            lambda: buf.at[j, far, pl.ds(0, 32)],
            lambda: buf.at[j, far, pl.ds(32, 32)],
            lambda: buf.at[j, other + y],
            lambda: buf.at[j, other + lax.rem(y + 3, 4)],
            lambda: buf.at[j, other + lax.rem(y + 1, 4)],
            lambda: buf.at[j, other + lax.rem(y + 2, 4)],
        )[n]()
        remote(block, block, ag_s.at[kind, j, n], ag_r.at[kind, j, n], partner).wait_recv()

    def gather_near(buf, kind, j):
        landed(buf, kind, j, 0)
        gather_copy(buf, kind, j, 2).start()
        gather_copy(buf, kind, j, 5).start()
        landed(buf, kind, j, 1)
        gather_copy(buf, kind, j, 3).start()
        gather_copy(buf, kind, j, 6).start()

    def gather_far(buf, kind, j):
        landed(buf, kind, j, 2)
        landed(buf, kind, j, 3)
        gather_copy(buf, kind, j, 7).start()

    def gather_rest(buf, kind, j):
        for n in (4, 5, 6, 7):
            landed(buf, kind, j, n)

    e_row = routing_ref[...]
    expert_t = iota((16, 128), 0) == e_row
    onehot_t = expert_t.astype(F32)
    before = (iota((128, 128), 0) < iota((128, 128), 1)).astype(BF16)
    earlier = mm(onehot_t.astype(BF16), before)
    slot = jnp.sum(earlier * onehot_t, axis=0, keepdims=True)
    high = (slot >= 4.0).astype(F32) + (slot >= 8.0).astype(F32)
    e_float = e_row.astype(F32)
    target = high * 252.0 + e_float * 16.0 + slot
    tgt_row[...] = target.astype(jnp.int32)
    eye128 = eye_mask(128)

    def to_column(row):
        return jnp.sum(jnp.where(eye128, row, 0.0), axis=1, keepdims=True)

    def to_row(column):
        return jnp.sum(jnp.where(eye128, column, 0.0), axis=0, keepdims=True)

    cols[0] = jnp.broadcast_to(to_column(target), (128, 128))
    cols[1] = jnp.broadcast_to(to_column(e_float), (128, 128))

    def fold_tokens(src, dst, j):
        total = None
        for g in range(GROUPS):
            place = (iota((256, 128), 0) == tgt_row[...] + (4 * g - 256 * j)).astype(BF16)
            term = mm(place, src[:, g * dgw : (g + 1) * dgw])
            total = term if total is None else total + term
        dst[j] = total.astype(BF16).reshape(16, 16, dgw)

    out_at = iota((256, 256), 0)
    in_at = iota((256, 256), 1)
    unfold_m[...] = (
        in_at == ((out_at >> 2) & 15) * 16 + (out_at >> 6) * 4 + (out_at & 3)
    ).astype(BF16)
    fold_m[...] = (
        in_at == ((out_at >> 2) & 3) * 64 + (out_at >> 4) * 4 + (out_at & 3)
    ).astype(BF16)

    loads[0].wait()
    for j in range(CHUNKS):
        fold_tokens(ogr, send_g, j)
        if j == 0:
            pl.semaphore_wait(barrier, 22)
        a2a_start(send_g, recv_g, 0, j)

    loads[1].wait()
    loads[2].wait()
    logits = mm(tok[...], rw[...])
    lane_e = iota((128, 16), 1).astype(F32)
    onehot = (lane_e == cols[1][:, :16]).astype(F32)
    score = jax.nn.sigmoid(jnp.sum(logits * onehot, axis=1, keepdims=True))
    cols[2] = jnp.broadcast_to(score, (128, 128))
    for g in range(GROUPS):
        part = slice(g * dgw, (g + 1) * dgw)
        scaled[:, part] = (score * tok[:, part].astype(F32)).astype(BF16)
    for j in range(CHUNKS):
        fold_tokens(scaled, send_i, j)
        a2a_start(send_i, recv_i, 1, j)

    save_out = iota((384, 384), 0)
    save_m[...] = (
        iota((384, 384), 1)
        == ((save_out >> 2) & 3) * 96
        + (((save_out >> 4) & 3) * 2 + ((save_out >> 6) & 1)) * 12
        + (save_out >> 7) * 4
        + (save_out & 3)
    ).astype(BF16)
    eye_m[...] = eye_mask(256).astype(BF16)
    loads[3].wait()
    loads[4].wait()

    def permute_saved(src, dst):
        @pl.loop(0, 4)
        def _(q):
            block = src[pl.ds(pl.multiple_of(q * 384, 384), 384), :]
            moved = mm(save_m[...], block).astype(BF16)
            for j in range(CHUNKS):
                for p in range(8):
                    start = (j * 8 + p) * 16
                    dst[j, pl.ds(pl.multiple_of(p * 64 + q * 16, 16), 16), :] = moved[
                        start : start + 16, :
                    ]

    permute_saved(ga, a_perm)
    permute_saved(gb, b_perm)

    def unfold(src, buf, j):
        moved = mm(unfold_m[...], src[j].reshape(256, dgw)).astype(BF16)
        for g in range(GROUPS):
            buf[j, mine, :, g * dgw : (g + 1) * dgw] = moved[g * 64 : (g + 1) * 64, :]

    def transposed(src_rows):
        return mm(eye_m[...], src_rows, NT).astype(BF16)

    def make_hidden(j):
        @pl.loop(0, 2)
        def _(n):
            at = pl.ds(pl.multiple_of(n * 256, 256), 256)
            a = a_perm[j, :, at].astype(F32)
            b = b_perm[j, :, at].astype(F32)
            hidden = (a * jax.nn.sigmoid(a) * b).astype(BF16)
            hid_t[j, at, :] = transposed(hidden)

    def compute(j):
        @pl.loop(0, 2)
        def _(n):
            at = pl.ds(pl.multiple_of(n * 256, 256), 256)
            gh = mm(full_g[j].reshape(rows, width), down[at, :], NT)
            a = a_perm[j, :, at].astype(F32)
            b = b_perm[j, :, at].astype(F32)
            sg = jax.nn.sigmoid(a)
            silu = a * sg
            here = pl.ds(j * 512, 512)
            ga[here, at] = (gh * b * sg * (1.0 + a * (1.0 - sg))).astype(BF16)
            gb[here, at] = (gh * silu).astype(BF16)

    def partial(j, parity, n):
        at = pl.ds(pl.multiple_of(j * 512 + parity * 256, 256), 256)
        hold = pl.ds(pl.multiple_of(n * dgw, 128), dgw)
        value = mm(ga[at, :], gate[hold, :], NT) + mm(gb[at, :], up[hold, :], NT)
        return value.astype(BF16).reshape(4, 64, dgw)

    def pair_copy(j):
        return remote(send_c, recv_c.at[j], pc_s.at[j], pc_r.at[j], partner)

    def partials(j):
        if j > 0:
            pair_copy(j - 1).wait_send()

        @pl.loop(0, GROUPS)
        def _(n):
            send_c[:, :, pl.ds(pl.multiple_of(n * dgw, 128), dgw)] = partial(j, 1 - c, n)

        pair_copy(j).start()

        @pl.loop(0, GROUPS)
        def _(n):
            own_p[j, :, :, pl.ds(pl.multiple_of(n * dgw, 128), dgw)] = partial(j, c, n)

    y_left = lax.rem(y + 3, 4)
    y_right = lax.rem(y + 1, 4)
    y_far = lax.rem(y + 2, 4)

    def pair_sum(j, at):
        return own_p[j, at].astype(F32) + recv_c[j, at].astype(F32)

    def rs_copy(j, n):
        src, dst, to = (
            (st1_s.at[0], st1_r.at[j, 0], right),
            (st1_s.at[1], st1_r.at[j, 1], left),
            (st2_s.at[0], st2_r.at[j, 0], right),
            (st2_s.at[1], st2_r.at[j, 1], left),
        )[n]
        return remote(src, dst, rs_s.at[j, n], rs_r.at[j, n], to)

    def reduce_far(j):
        pair_copy(j).wait_recv()
        if j > 0:
            rs_copy(j - 1, 0).wait_send()
            rs_copy(j - 1, 1).wait_send()
        total = pair_sum(j, y_far)
        st1_s[0] = total[:32].astype(BF16)
        st1_s[1] = total[32:].astype(BF16)
        rs_copy(j, 0).start()
        rs_copy(j, 1).start()

    def reduce_near(j):
        if j > 0:
            rs_copy(j - 1, 2).wait_send()
            rs_copy(j - 1, 3).wait_send()
        rs_copy(j, 0).wait_recv()
        total = pair_sum(j, y_right)
        st2_s[0, :32] = (total[:32] + st1_r[j, 0].astype(F32)).astype(BF16)
        st2_s[0, 32:] = total[32:].astype(BF16)
        rs_copy(j, 2).start()
        rs_copy(j, 1).wait_recv()
        total = pair_sum(j, y_left)
        st2_s[1, :32] = total[:32].astype(BF16)
        st2_s[1, 32:] = (total[32:] + st1_r[j, 1].astype(F32)).astype(BF16)
        rs_copy(j, 3).start()

    def reduce_last(j):
        rs_copy(j, 2).wait_recv()
        rs_copy(j, 3).wait_recv()
        total = pair_sum(j, y) + st2_r[j, 0].astype(F32) + st2_r[j, 1].astype(F32)
        total = total.astype(BF16)
        stacked = jnp.concatenate(
            [total[:, g * dgw : (g + 1) * dgw] for g in range(GROUPS)], axis=0
        )
        a2a_drain(send_g, 0, j)
        send_g[j] = mm(fold_m[...], stacked).astype(BF16).reshape(16, 16, dgw)
        a2a_start(send_g, recv_r, 2, j)

    def own_rows(src, buf, kind, j):
        a2a_wait(src, kind, j)
        unfold(src, buf, j)
        gather_own(buf, kind, j)

    own_rows(recv_g, full_g, 0, 0)
    own_rows(recv_g, full_g, 0, 1)
    make_hidden(0)
    gather_near(full_g, 0, 0)
    own_rows(recv_g, full_g, 0, 2)
    make_hidden(1)
    gather_far(full_g, 0, 0)
    gather_near(full_g, 0, 1)
    make_hidden(2)
    for load in loads[5:]:
        load.wait()
    gather_rest(full_g, 0, 0)
    compute(0)
    gather_near(full_g, 0, 2)
    partials(0)
    gather_far(full_g, 0, 1)
    reduce_far(0)
    own_rows(recv_i, full_i, 1, 0)
    gather_far(full_g, 0, 2)
    gather_rest(full_g, 0, 1)
    compute(1)
    partials(1)
    reduce_far(1)
    reduce_near(0)
    gather_rest(full_g, 0, 2)
    compute(2)
    partials(2)
    reduce_far(2)
    reduce_near(1)
    reduce_last(0)
    gather_near(full_i, 1, 0)
    reduce_near(2)
    own_rows(recv_i, full_i, 1, 1)
    own_rows(recv_i, full_i, 1, 2)

    def transpose_grads(j):
        @pl.loop(0, 2)
        def _(n):
            at = pl.ds(pl.multiple_of(n * 256, 256), 256)
            here = pl.ds(j * 512, 512)
            a_perm[j, at, :] = transposed(ga[here, at])
            b_perm[j, at, :] = transposed(gb[here, at])

    for j in range(CHUNKS):
        transpose_grads(j)

    reduce_last(1)

    tile = 512

    @pl.loop(0, width // tile)
    def _(n):
        at = pl.ds(pl.multiple_of(n * tile, tile), tile)
        total = None
        for j in range(CHUNKS):
            term = mm(hid_t[j], full_g[j, :, :, at].reshape(rows, tile))
            total = term if total is None else total + term
        down[:, at] = total.astype(BF16)

    down_out = pltpu.make_async_copy(down, grad_down_hbm, out_sem.at[0])
    down_out.start()

    gather_far(full_i, 1, 0)
    reduce_last(2)
    gather_near(full_i, 1, 1)

    def bring_back(j):
        a2a_wait(recv_r, 2, j)
        for g in range(GROUPS):
            part = slice(g * dgw, (g + 1) * dgw)
            wanted = cols[0].astype(jnp.int32)
            wanted = jnp.concatenate([wanted, wanted], axis=1) + (4 * g - 256 * j)
            take = (iota((128, 256), 1) == wanted).astype(BF16)
            moved = mm(take, recv_r[j].reshape(256, dgw))
            if j == 0:
                gs[:, part] = moved
            else:
                gs[:, part] += moved

    for j in range(CHUNKS):
        bring_back(j)
    score = cols[2][:, :1]
    grad_score = jnp.zeros((128, 1), F32)
    for g in range(GROUPS):
        part = slice(g * dgw, (g + 1) * dgw)
        grad_score += jnp.sum(tok[:, part].astype(F32) * gs[:, part], axis=1, keepdims=True)
    grad_logit = grad_score * score * (1.0 - score)
    lane_e = iota((128, 16), 1).astype(F32)
    onehot = (lane_e == cols[1][:, :16]).astype(BF16)
    expert_t = iota((16, 128), 0) == routing_ref[...]
    weight_t = jnp.where(expert_t, to_row(grad_logit), 0.0)
    w_high = weight_t.astype(BF16)
    rest = weight_t - w_high.astype(F32)
    w_mid = rest.astype(BF16)
    w_low = (rest - w_mid.astype(F32)).astype(BF16)
    weights3 = jnp.concatenate([w_high, w_mid, w_low], axis=0)
    for g in range(GROUPS):
        part = slice(g * dgw, (g + 1) * dgw)
        share = mm(weights3, tok[:, part])
        share = share[:16] + share[16:32] + share[32:]
        rp_s[g] = share[:8]
        rp_s[4 + g] = share[8:]

    def all_tensor(src, dst, n, whole):
        @pl.loop(1, 8)
        def _(k):
            to = lax.rem(t + k, 8)
            block = src if whole else src.at[to]
            remote(block, dst.at[t], rt_s.at[n], rt_r.at[n], (d, to)).start()

    def wait_tensor(dst, n, sem):
        block = dst.at[pl.ds(0, 7)]
        pltpu.make_async_copy(block, block, sem.at[n]).wait()

    all_tensor(rp_s, rp_r, 0, False)
    rp_r[t] = rp_s[t]

    for g in range(GROUPS):
        part = slice(g * dgw, (g + 1) * dgw)
        picked = mm(onehot, rw[part, :], NT)
        ogr[:, part] = (score * gs[:, part] + grad_logit * picked).astype(BF16)
    tokens_out = pltpu.make_async_copy(ogr, grad_tokens_hbm, out_sem.at[1])
    tokens_out.start()

    wait_tensor(rp_r, 0, rt_r)
    rd_s[...] = jnp.sum(rp_r[...], axis=0)

    @pl.loop(1, 16)
    def _(k):
        to = lax.rem(d + k, 16)
        remote(rd_s, rd_r.at[d], rt_s.at[1], rt_r.at[1], (to, t)).start()

    rd_r[d] = rd_s[...]

    gather_far(full_i, 1, 1)
    gather_near(full_i, 1, 2)

    block = rd_r.at[pl.ds(0, 15)]
    pltpu.make_async_copy(block, block, rt_r.at[1]).wait()
    ro_s[...] = jnp.sum(rd_r[...], axis=0)
    all_tensor(ro_s, ro_r, 2, True)
    ro_r[t] = ro_s[...]
    gather_far(full_i, 1, 2)
    wait_tensor(ro_r, 2, rt_r)
    for g in range(GROUPS):
        part = slice(g * dgw, (g + 1) * dgw)
        grad_router_ref[:8, part] = ro_r[g]
        grad_router_ref[8:, part] = ro_r[4 + g]

    for j in range(CHUNKS):
        gather_rest(full_i, 1, j)

    @pl.loop(0, width // 256)
    def _(n):
        at = pl.ds(pl.multiple_of(n * 256, 256), 256)
        for src, dst, hbm, k in ((a_perm, gate, grad_gate_hbm, 2), (b_perm, up, grad_up_hbm, 3)):
            total = None
            for j in range(CHUNKS):
                term = mm(src[j], full_i[j, :, :, at].reshape(rows, 256))
                total = term if total is None else total + term
            dst[at, :] = transposed(total.astype(BF16))
            pltpu.make_async_copy(dst.at[at, :], hbm.at[at, :], out_sem.at[k]).start()

    down_out.wait()
    tokens_out.wait()
    pltpu.make_async_copy(gate, grad_gate_hbm, out_sem.at[2]).wait()
    pltpu.make_async_copy(up, grad_up_hbm, out_sem.at[3]).wait()
    for j in range(CHUNKS):
        a2a_drain(send_i, 1, j)
        a2a_drain(send_g, 2, j)
        for n in range(8):
            gather_copy(full_g, 0, j, n).wait_send()
            gather_copy(full_i, 1, j, n).wait_send()
    pair_copy(CHUNKS - 1).wait_send()
    for n in range(4):
        rs_copy(CHUNKS - 1, n).wait_send()
    wait_tensor(rp_s, 0, rt_s)
    block = rd_r.at[pl.ds(0, 15)]
    pltpu.make_async_copy(block, block, rt_s.at[1]).wait()
    wait_tensor(ro_r, 2, rt_s)


def local(
    tokens,
    out_grad,
    routing,
    router_weight,
    gate_weight,
    up_weight,
    down_weight,
    saved_gate,
    saved_up,
):
    count, width = tokens.shape
    experts = router_weight.shape[1]
    slots = saved_gate.shape[1]
    hidden = saved_gate.shape[2]
    per = slots // CHUNKS
    dgw = width // GROUPS
    anywhere = pl.BlockSpec(memory_space=pl.ANY)
    vmem = pl.BlockSpec(memory_space=pltpu.VMEM)
    dma = pltpu.SemaphoreType.DMA
    folded = pltpu.VMEM((CHUNKS, experts, 16, dgw), BF16)
    outs = pl.pallas_call(
        kernel,
        out_shape=(
            jax.ShapeDtypeStruct((count, width), BF16),
            jax.ShapeDtypeStruct((width, hidden), BF16),
            jax.ShapeDtypeStruct((width, hidden), BF16),
            jax.ShapeDtypeStruct((hidden, width), BF16),
            jax.ShapeDtypeStruct((experts, width), F32),
        ),
        in_specs=[vmem] + [anywhere] * 8,
        out_specs=(anywhere, anywhere, anywhere, anywhere, vmem),
        scratch_shapes=[
            pltpu.VMEM((count, width), BF16),
            pltpu.VMEM((count, width), BF16),
            pltpu.VMEM((count, width), BF16),
            pltpu.VMEM((width, experts), BF16),
            pltpu.VMEM((width, hidden), BF16),
            pltpu.VMEM((width, hidden), BF16),
            pltpu.VMEM((hidden, width), BF16),
            pltpu.VMEM((CHUNKS, per, hidden), BF16),
            pltpu.VMEM((CHUNKS, per, hidden), BF16),
            pltpu.VMEM((CHUNKS, hidden, per), BF16),
            pltpu.VMEM((slots, hidden), BF16),
            pltpu.VMEM((slots, hidden), BF16),
            folded,
            folded,
            folded,
            folded,
            folded,
            pltpu.VMEM((CHUNKS, 8, 64, width), BF16),
            pltpu.VMEM((CHUNKS, 8, 64, width), BF16),
            pltpu.VMEM((4, 64, width), BF16),
            pltpu.VMEM((CHUNKS, 4, 64, width), BF16),
            pltpu.VMEM((CHUNKS, 4, 64, width), BF16),
            pltpu.VMEM((2, 32, width), BF16),
            pltpu.VMEM((CHUNKS, 2, 32, width), BF16),
            pltpu.VMEM((2, 64, width), BF16),
            pltpu.VMEM((CHUNKS, 2, 64, width), BF16),
            pltpu.VMEM((256, 256), BF16),
            pltpu.VMEM((256, 256), BF16),
            pltpu.VMEM((384, 384), BF16),
            pltpu.VMEM((256, 256), BF16),
            pltpu.VMEM((count, width), F32),
            pltpu.VMEM((1, 128), jnp.int32),
            pltpu.VMEM((3, 128, 128), F32),
            pltpu.VMEM((8, 8, dgw), F32),
            pltpu.VMEM((8, 8, dgw), F32),
            pltpu.VMEM((8, dgw), F32),
            pltpu.VMEM((16, 8, dgw), F32),
            pltpu.VMEM((8, dgw), F32),
            pltpu.VMEM((8, 8, dgw), F32),
            dma((8,)),
            dma((3, CHUNKS)),
            dma((3, CHUNKS)),
            dma((2, CHUNKS, 8)),
            dma((2, CHUNKS, 8)),
            dma((CHUNKS,)),
            dma((CHUNKS,)),
            dma((CHUNKS, 4)),
            dma((CHUNKS, 4)),
            dma((3,)),
            dma((3,)),
            dma((4,)),
        ],
        compiler_params=pltpu.CompilerParams(
            collective_id=0, has_side_effects=True, vmem_limit_bytes=63 * 2**20
        ),
        cost_estimate=pl.CostEstimate(
            flops=12 * slots * width * hidden,
            bytes_accessed=2 * (6 * width * hidden + 2 * slots * hidden + 4 * count * width),
            transcendentals=slots * hidden,
        ),
    )(
        routing.reshape(1, count),
        tokens,
        out_grad,
        router_weight,
        gate_weight[0],
        up_weight[0],
        down_weight[0],
        saved_gate[0],
        saved_up[0],
    )
    grad_tokens, grad_gate, grad_up, grad_down, grad_router = outs
    return grad_tokens, grad_gate[None], grad_up[None], grad_down[None], grad_router.T


def solution(mesh):
    placed = (
        P(("dp", "tensor"), None),
        P(("dp", "tensor"), None),
        P(("dp", "tensor"), None),
        P(),
        P("dp", None, "tensor"),
        P("dp", None, "tensor"),
        P("dp", "tensor", None),
        P("dp", None, "tensor"),
        P("dp", None, "tensor"),
    )
    return jax.shard_map(
        local,
        mesh=mesh,
        in_specs=placed,
        out_specs=(
            P(("dp", "tensor"), None),
            P("dp", None, "tensor"),
            P("dp", None, "tensor"),
            P("dp", "tensor", None),
            P(),
        ),
        check_vma=False,
    )
```

time: 642 us -> 163 us (0.25)
  waiting for transfers between devices: 339 us -> 0 us
  Pallas kernels: 0 us -> 150 us
  blocking collectives: 133 us -> 0 us
  matrix products: 69.1 us -> 0 us
  local copies, waits for them, and re-layouts: 58.3 us -> 12.3 us
  starting transfers between devices: 18.9 us -> 0 us
  between operations: 14.1 us -> 0.65 us
  other arithmetic: 8.21 us -> 0 us
    all_to_all x2 -> x0, waiting for transfers between devices: 254 us -> none  [the longest x1 132 us: local(): lax.all_to_all(pieces, ('dp', 'tensor'), split_axis=0, concat_axis=0, til...]
    pallas_call x0 -> x1, Pallas kernels: none -> 150 us  [local(): pl.pallas_call(kernel, out_shape=(jax.ShapeDtypeStruct((count, width), BF...]
    all_to_all x1 -> x0, blocking collectives: 133 us -> none  [local(): lax.all_to_all(spread_grad, ('dp', 'tensor'), split_axis=0, concat_axis=0...]
    psum x1 -> x0, waiting for transfers between devices: 84.6 us -> none  [local(): grad_router = lax.psum(router_part, ('dp', 'tensor'))]
    dot_general x12 -> x0, matrix products: 69.1 us -> none  [the longest x1 15.3 us: local(): lax.dot_general(grad_b, up_weight[0], hidden_dims, preferred_element_type...]
    reshape x4 -> x0, local copies, waits for them, and re-layouts: 39.3 us -> none  [the longest x1 12.8 us: local(): expert_grad = got_grad.reshape(slot_total, features)]
    all_to_all x2 -> x0, starting transfers between devices: 18.8 us -> none  [the longest x1 10 us: local(): lax.all_to_all(pieces, ('dp', 'tensor'), split_axis=0, concat_axis=0, til...]
    broadcast_in_dim x4 -> x0, local copies, waits for them, and re-layouts: 17.3 us -> none  [the longest x2 8.64 us: local(): jnp.broadcast_to(send_in[:, None], (experts, group_count, capacity, featu...]
  transfers between devices with their start and end apart: 3 -> 0, of which waited for: 3 -> 0; matrix products, arithmetic and copies ran while one was open for 6% -> 0% of each run, Pallas kernels for 0% -> 0%
where the time goes in v1:
time: 163 us
  Pallas kernels  150 us (92%)
  local copies, waits for them, and re-layouts  12.3 us (8%)
    pallas_call x1, Pallas kernels, local(): pl.pallas_call(kernel, out_shape=(jax.ShapeDtypeStruct((count, width), BF...  150 us
    unnamed x12, local copies, waits for them, and re-layouts  12.3 us

profile of v1, /device:TPU:1, one launch (start us, length us, event | category | flops | bytes accessed | tf_op | source)
XLA Modules:
  0.0 163.3 jit_solution(6643534007179574373)
XLA Ops:
  0.6 2.0 %copy.14.router_hbm = bf16[2560,16]{1,0:T(8,128)(2,1)} copy(bf16[2560,16]{0,1:T(8,128)(2,1)} %param.12) | data formatting | bytes 163840 | tf_op args[3]
  2.6 150.3 %shard_map.128 = (bf16[128,2560]{1,0:T(8,128)(2,1)}, bf16[2560,512]{1,0:T(8,128)(2,1)}, bf16[2560,512]{1,0:T(8,128)(2,1)}, bf16[512,2560]{1,0:T(8,128)(2,1)}, f32[16,2560]{1,0:T(8,128)}) custom-call(s32[1,128]{1,0:T(1,128)} %bitcast.19, bf16[128,2560]{1,0:T(8,128)(2,1)} %tokens_hbm.1, bf16[128,2560]{1,0:T(8,128)(2,1)} %out_grad_hbm.1, ...), custom_call_target="tpu_custom_call" | custom-call | flops 24159191040 | bytes 21495808 | tf_op jit(solution)/shard_map/pallas_call | solution.py:621
  152.9 2.0 %copy.20 = bf16[128,2560]{1,0:T(8,128)(2,1)} copy(bf16[128,2560]{1,0:T(8,128)(2,1)} %get-tuple-element.20) | data formatting | bytes 1310720
  154.8 0.0 copy-start.1
  154.9 3.6 %copy.21 = bf16[1,2560,512]{2,1,0:T(8,128)(2,1)} copy(bf16[1,2560,512]{2,1,0:T(8,128)(2,1)} %bitcast.12) | data formatting | bytes 5242880
  158.4 0.0 copy-done.1
  158.4 0.0 copy-start
  158.4 1.5 copy.22
  159.9 1.2 copy-done
  161.1 0.0 copy-start.2
  161.1 1.5 copy.23
  162.6 0.0 copy-done.2
  162.6 0.7 copy.24
Async XLA Ops:
  154.8 3.6 %copy-start.1 = (bf16[2560,512]{1,0:T(8,128)(2,1)S(1)}, bf16[2560,512]{1,0:T(8,128)(2,1)}, u32[]{:S(2)}) copy-start(bf16[2560,512]{1,0:T(8,128)(2,1)} %get-tuple-element.12) | copy-start | bytes 7864324
  158.4 2.7 %copy-start = (bf16[512,2560]{1,0:T(8,128)(2,1)S(1)}, bf16[512,2560]{1,0:T(8,128)(2,1)}, u32[]{:S(2)}) copy-start(bf16[512,2560]{1,0:T(8,128)(2,1)} %get-tuple-element.13) | copy-start | bytes 7864324
  161.1 1.5 copy-start.2

commit v2 on v1

--- a/solution.py
+++ b/solution.py
@@ -8,6 +8,7 @@
 MESH = pl.DeviceIdType.MESH
 NN = (((1,), (0,)), ((), ()))
 NT = (((1,), (1,)), ((), ()))
+TN = (((0,), (0,)), ((), ()))
 F32 = jnp.float32
 BF16 = jnp.bfloat16
 
@@ -38,22 +39,22 @@
     saved_gate_hbm,
     saved_up_hbm,
     grad_tokens_hbm,
-    grad_gate_hbm,
-    grad_up_hbm,
+    early_hbm,
+    late_in_hbm,
+    late_grad_hbm,
     grad_down_hbm,
     grad_router_ref,
     tok,
     ogr,
-    scaled,
+    tok_rows,
+    row_score,
     rw,
-    gate,
-    up,
+    weights,
     down,
     a_perm,
     b_perm,
     hid_t,
-    ga,
-    gb,
+    gab,
     send_g,
     send_i,
     recv_g,
@@ -71,16 +72,13 @@
     unfold_m,
     fold_m,
     save_m,
-    eye_m,
     gs,
     tgt_row,
     cols,
-    rp_s,
-    rp_r,
-    rd_s,
-    rd_r,
-    ro_s,
-    ro_r,
+    rx_s,
+    rx_r,
+    ry_s,
+    ry_r,
     load_sem,
     a2a_s,
     a2a_r,
@@ -108,6 +106,7 @@
     dgw = tok.shape[1] // GROUPS
     rows = full_g.shape[1] * full_g.shape[2]
     width = tok.shape[1]
+    hidden = down.shape[0]
 
     loads = [
         pltpu.make_async_copy(src, dst, load_sem.at[n])
@@ -116,15 +115,15 @@
                 (out_grad_hbm, ogr),
                 (tokens_hbm, tok),
                 (router_hbm, rw),
-                (saved_gate_hbm, ga),
-                (saved_up_hbm, gb),
+                (saved_gate_hbm, gab.at[:, pl.ds(0, hidden)]),
+                (saved_up_hbm, gab.at[:, pl.ds(hidden, hidden)]),
                 (down_hbm, down),
-                (gate_hbm, gate),
-                (up_hbm, up),
+                (gate_hbm, weights.at[:, pl.ds(0, hidden)]),
+                (up_hbm, weights.at[:, pl.ds(hidden, hidden)]),
             )
         )
     ]
-    for load in loads:
+    for load in loads[:3]:
         load.start()
 
     barrier = pltpu.get_barrier_semaphore()
@@ -255,27 +254,6 @@
         in_at == ((out_at >> 2) & 3) * 64 + (out_at >> 4) * 4 + (out_at & 3)
     ).astype(BF16)
 
-    loads[0].wait()
-    for j in range(CHUNKS):
-        fold_tokens(ogr, send_g, j)
-        if j == 0:
-            pl.semaphore_wait(barrier, 22)
-        a2a_start(send_g, recv_g, 0, j)
-
-    loads[1].wait()
-    loads[2].wait()
-    logits = mm(tok[...], rw[...])
-    lane_e = iota((128, 16), 1).astype(F32)
-    onehot = (lane_e == cols[1][:, :16]).astype(F32)
-    score = jax.nn.sigmoid(jnp.sum(logits * onehot, axis=1, keepdims=True))
-    cols[2] = jnp.broadcast_to(score, (128, 128))
-    for g in range(GROUPS):
-        part = slice(g * dgw, (g + 1) * dgw)
-        scaled[:, part] = (score * tok[:, part].astype(F32)).astype(BF16)
-    for j in range(CHUNKS):
-        fold_tokens(scaled, send_i, j)
-        a2a_start(send_i, recv_i, 1, j)
-
     save_out = iota((384, 384), 0)
     save_m[...] = (
         iota((384, 384), 1)
@@ -284,60 +262,50 @@
         + (save_out >> 7) * 4
         + (save_out & 3)
     ).astype(BF16)
-    eye_m[...] = eye_mask(256).astype(BF16)
-    loads[3].wait()
-    loads[4].wait()
-
-    def permute_saved(src, dst):
+    def permute_saved(start, dst):
         @pl.loop(0, 4)
         def _(q):
-            block = src[pl.ds(pl.multiple_of(q * 384, 384), 384), :]
+            block = gab[pl.ds(pl.multiple_of(q * 384, 384), 384), start : start + hidden]
             moved = mm(save_m[...], block).astype(BF16)
             for j in range(CHUNKS):
                 for p in range(8):
-                    start = (j * 8 + p) * 16
+                    first = (j * 8 + p) * 16
                     dst[j, pl.ds(pl.multiple_of(p * 64 + q * 16, 16), 16), :] = moved[
-                        start : start + 16, :
+                        first : first + 16, :
                     ]
-
-    permute_saved(ga, a_perm)
-    permute_saved(gb, b_perm)
 
     def unfold(src, buf, j):
         moved = mm(unfold_m[...], src[j].reshape(256, dgw)).astype(BF16)
         for g in range(GROUPS):
             buf[j, mine, :, g * dgw : (g + 1) * dgw] = moved[g * 64 : (g + 1) * 64, :]
 
-    def transposed(src_rows):
-        return mm(eye_m[...], src_rows, NT).astype(BF16)
-
     def make_hidden(j):
-        @pl.loop(0, 2)
+        @pl.loop(0, hidden // 256)
         def _(n):
             at = pl.ds(pl.multiple_of(n * 256, 256), 256)
             a = a_perm[j, :, at].astype(F32)
             b = b_perm[j, :, at].astype(F32)
-            hidden = (a * jax.nn.sigmoid(a) * b).astype(BF16)
-            hid_t[j, at, :] = transposed(hidden)
+            value = (a * jax.nn.sigmoid(a) * b).astype(BF16)
+            hid_t[at, j * rows : (j + 1) * rows] = value.T
 
     def compute(j):
-        @pl.loop(0, 2)
+        @pl.loop(0, hidden // 256)
         def _(n):
             at = pl.ds(pl.multiple_of(n * 256, 256), 256)
+            too = pl.ds(pl.multiple_of(n * 256 + hidden, 256), 256)
             gh = mm(full_g[j].reshape(rows, width), down[at, :], NT)
             a = a_perm[j, :, at].astype(F32)
             b = b_perm[j, :, at].astype(F32)
             sg = jax.nn.sigmoid(a)
             silu = a * sg
-            here = pl.ds(j * 512, 512)
-            ga[here, at] = (gh * b * sg * (1.0 + a * (1.0 - sg))).astype(BF16)
-            gb[here, at] = (gh * silu).astype(BF16)
+            here = pl.ds(j * rows, rows)
+            gab[here, at] = (gh * b * sg * (1.0 + a * (1.0 - sg))).astype(BF16)
+            gab[here, too] = (gh * silu).astype(BF16)
 
     def partial(j, parity, n):
-        at = pl.ds(pl.multiple_of(j * 512 + parity * 256, 256), 256)
+        at = pl.ds(pl.multiple_of(j * rows + parity * 256, 256), 256)
         hold = pl.ds(pl.multiple_of(n * dgw, 128), dgw)
-        value = mm(ga[at, :], gate[hold, :], NT) + mm(gb[at, :], up[hold, :], NT)
-        return value.astype(BF16).reshape(4, 64, dgw)
+        return mm(gab[at, :], weights[hold, :], NT).astype(BF16).reshape(4, 64, dgw)
 
     def pair_copy(j):
         return remote(send_c, recv_c.at[j], pc_s.at[j], pc_r.at[j], partner)
@@ -403,6 +371,15 @@
         rs_copy(j, 3).wait_recv()
         total = pair_sum(j, y) + st2_r[j, 0].astype(F32) + st2_r[j, 1].astype(F32)
         total = total.astype(BF16)
+        token = tok_rows[j].astype(F32)
+        score = row_score[j][:, :1]
+        grad_score = jnp.sum(token * total.astype(F32), axis=1, keepdims=True)
+        grad_logit = grad_score * score * (1.0 - score)
+        share = jnp.sum(token * grad_logit, axis=0, keepdims=True)
+        if j == 0:
+            rx_s[...] = share
+        else:
+            rx_s[...] += share
         stacked = jnp.concatenate(
             [total[:, g * dgw : (g + 1) * dgw] for g in range(GROUPS)], axis=0
         )
@@ -410,76 +387,106 @@
         send_g[j] = mm(fold_m[...], stacked).astype(BF16).reshape(16, 16, dgw)
         a2a_start(send_g, recv_r, 2, j)
 
-    def own_rows(src, buf, kind, j):
-        a2a_wait(src, kind, j)
-        unfold(src, buf, j)
-        gather_own(buf, kind, j)
-
-    own_rows(recv_g, full_g, 0, 0)
-    own_rows(recv_g, full_g, 0, 1)
-    make_hidden(0)
+    def own_grads(j):
+        a2a_wait(recv_g, 0, j)
+        moved = mm(unfold_m[...], recv_g[j].reshape(256, dgw)).astype(BF16)
+        for g in range(GROUPS):
+            full_g[j, mine, :, g * dgw : (g + 1) * dgw] = moved[g * 64 : (g + 1) * 64, :]
+        gather_own(full_g, 0, j)
+
+    def own_inputs(j):
+        a2a_wait(recv_i, 1, j)
+        moved = mm(unfold_m[...], recv_i[j].reshape(256, dgw)).astype(BF16)
+        for g in range(GROUPS):
+            tok_rows[j, :, g * dgw : (g + 1) * dgw] = moved[g * 64 : (g + 1) * 64, :]
+        logits = mm(tok_rows[j], rw[...], NT)
+        logit = jnp.sum(jnp.where(iota((64, 16), 1) == d, logits, 0.0), axis=1, keepdims=True)
+        score = jax.nn.sigmoid(logit)
+        row_score[j] = jnp.broadcast_to(score, (64, 128))
+        full_i[j, mine] = (score * tok_rows[j].astype(F32)).astype(BF16)
+
+    loads[0].wait()
+    for j in range(CHUNKS):
+        fold_tokens(ogr, send_g, j)
+        if j == 0:
+            pl.semaphore_wait(barrier, 22)
+        a2a_start(send_g, recv_g, 0, j)
+    for load in loads[3:]:
+        load.start()
+    loads[1].wait()
+    for j in range(CHUNKS):
+        own_grads(j)
+        fold_tokens(tok, send_i, j)
+        a2a_start(send_i, recv_i, 1, j)
     gather_near(full_g, 0, 0)
-    own_rows(recv_g, full_g, 0, 2)
-    make_hidden(1)
+    loads[3].wait()
+    loads[4].wait()
+    permute_saved(0, a_perm)
+    gather_near(full_g, 0, 1)
+    permute_saved(hidden, b_perm)
     gather_far(full_g, 0, 0)
-    gather_near(full_g, 0, 1)
-    make_hidden(2)
     for load in loads[5:]:
         load.wait()
+    loads[2].wait()
+    own_inputs(0)
+    gather_near(full_g, 0, 2)
+    gather_own(full_i, 1, 0)
     gather_rest(full_g, 0, 0)
     compute(0)
-    gather_near(full_g, 0, 2)
+    gather_far(full_g, 0, 1)
     partials(0)
-    gather_far(full_g, 0, 1)
+    gather_far(full_g, 0, 2)
     reduce_far(0)
-    own_rows(recv_i, full_i, 1, 0)
-    gather_far(full_g, 0, 2)
     gather_rest(full_g, 0, 1)
     compute(1)
     partials(1)
+    reduce_near(0)
     reduce_far(1)
-    reduce_near(0)
     gather_rest(full_g, 0, 2)
     compute(2)
+    gather_near(full_i, 1, 0)
     partials(2)
+    reduce_near(1)
     reduce_far(2)
-    reduce_near(1)
+    own_inputs(1)
+    gather_own(full_i, 1, 1)
     reduce_last(0)
-    gather_near(full_i, 1, 0)
+    own_inputs(2)
+    late_grad = pltpu.make_async_copy(
+        gab.at[pl.ds(2 * rows, rows)], late_grad_hbm, out_sem.at[4]
+    )
+    late_grad.start()
+    make_hidden(0)
+    make_hidden(1)
+    make_hidden(2)
+    logits = mm(tok[...], rw[...], NT)
+    lane_e = iota((128, 16), 1).astype(F32)
+    onehot = (lane_e == cols[1][:, :16]).astype(F32)
+    score = jax.nn.sigmoid(jnp.sum(logits * onehot, axis=1, keepdims=True))
+    cols[2] = jnp.broadcast_to(score, (128, 128))
     reduce_near(2)
-    own_rows(recv_i, full_i, 1, 1)
-    own_rows(recv_i, full_i, 1, 2)
-
-    def transpose_grads(j):
-        @pl.loop(0, 2)
-        def _(n):
-            at = pl.ds(pl.multiple_of(n * 256, 256), 256)
-            here = pl.ds(j * 512, 512)
-            a_perm[j, at, :] = transposed(ga[here, at])
-            b_perm[j, at, :] = transposed(gb[here, at])
-
-    for j in range(CHUNKS):
-        transpose_grads(j)
-
-    reduce_last(1)
+    gather_far(full_i, 1, 0)
 
     tile = 512
 
     @pl.loop(0, width // tile)
     def _(n):
         at = pl.ds(pl.multiple_of(n * tile, tile), tile)
-        total = None
-        for j in range(CHUNKS):
-            term = mm(hid_t[j], full_g[j, :, :, at].reshape(rows, tile))
-            total = term if total is None else total + term
-        down[:, at] = total.astype(BF16)
+        down[:, at] = mm(hid_t[...], full_g[:, :, :, at].reshape(CHUNKS * rows, tile)).astype(BF16)
 
     down_out = pltpu.make_async_copy(down, grad_down_hbm, out_sem.at[0])
     down_out.start()
-
-    gather_far(full_i, 1, 0)
+    reduce_last(1)
+    gather_near(full_i, 1, 1)
+    gather_own(full_i, 1, 2)
     reduce_last(2)
-    gather_near(full_i, 1, 1)
+
+    @pl.loop(1, 8)
+    def _(k):
+        to = lax.rem(t + k, 8)
+        remote(rx_s, rx_r.at[t], rt_s.at[0], rt_r.at[0], (d, to)).start()
+
+    rx_r[t] = rx_s[...]
 
     def bring_back(j):
         a2a_wait(recv_r, 2, j)
@@ -494,8 +501,10 @@
             else:
                 gs[:, part] += moved
 
-    for j in range(CHUNKS):
-        bring_back(j)
+    bring_back(0)
+    bring_back(1)
+    gather_far(full_i, 1, 1)
+    bring_back(2)
     score = cols[2][:, :1]
     grad_score = jnp.zeros((128, 1), F32)
     for g in range(GROUPS):
@@ -504,84 +513,57 @@
     grad_logit = grad_score * score * (1.0 - score)
     lane_e = iota((128, 16), 1).astype(F32)
     onehot = (lane_e == cols[1][:, :16]).astype(BF16)
-    expert_t = iota((16, 128), 0) == routing_ref[...]
-    weight_t = jnp.where(expert_t, to_row(grad_logit), 0.0)
-    w_high = weight_t.astype(BF16)
-    rest = weight_t - w_high.astype(F32)
-    w_mid = rest.astype(BF16)
-    w_low = (rest - w_mid.astype(F32)).astype(BF16)
-    weights3 = jnp.concatenate([w_high, w_mid, w_low], axis=0)
     for g in range(GROUPS):
         part = slice(g * dgw, (g + 1) * dgw)
-        share = mm(weights3, tok[:, part])
-        share = share[:16] + share[16:32] + share[32:]
-        rp_s[g] = share[:8]
-        rp_s[4 + g] = share[8:]
-
-    def all_tensor(src, dst, n, whole):
-        @pl.loop(1, 8)
-        def _(k):
-            to = lax.rem(t + k, 8)
-            block = src if whole else src.at[to]
-            remote(block, dst.at[t], rt_s.at[n], rt_r.at[n], (d, to)).start()
-
-    def wait_tensor(dst, n, sem):
-        block = dst.at[pl.ds(0, 7)]
-        pltpu.make_async_copy(block, block, sem.at[n]).wait()
-
-    all_tensor(rp_s, rp_r, 0, False)
-    rp_r[t] = rp_s[t]
-
-    for g in range(GROUPS):
-        part = slice(g * dgw, (g + 1) * dgw)
-        picked = mm(onehot, rw[part, :], NT)
+        picked = mm(onehot, rw[:, part])
         ogr[:, part] = (score * gs[:, part] + grad_logit * picked).astype(BF16)
     tokens_out = pltpu.make_async_copy(ogr, grad_tokens_hbm, out_sem.at[1])
     tokens_out.start()
 
-    wait_tensor(rp_r, 0, rt_r)
-    rd_s[...] = jnp.sum(rp_r[...], axis=0)
+    block = rx_r.at[pl.ds(0, 7)]
+    pltpu.make_async_copy(block, block, rt_r.at[0]).wait()
+    ry_s[...] = jnp.sum(rx_r[...], axis=0)
 
     @pl.loop(1, 16)
     def _(k):
         to = lax.rem(d + k, 16)
-        remote(rd_s, rd_r.at[d], rt_s.at[1], rt_r.at[1], (to, t)).start()
-
-    rd_r[d] = rd_s[...]
-
-    gather_far(full_i, 1, 1)
+        remote(ry_s, ry_r.at[d], rt_s.at[1], rt_r.at[1], (to, t)).start()
+
+    ry_r[d] = ry_s[...]
+
+    def early(first, last):
+        @pl.loop(first, last)
+        def _(n):
+            at = pl.ds(pl.multiple_of(n * 256, 256), 256)
+            value = mm(full_i[:2, :, :, at].reshape(2 * rows, 256), gab[: 2 * rows, :], TN)
+            weights[at, :] = value.astype(BF16)
+            pltpu.make_async_copy(
+                weights.at[at, :], early_hbm.at[at, :], out_sem.at[2]
+            ).start()
+
+    def late_in(p):
+        pltpu.make_async_copy(full_i.at[2, p], late_in_hbm.at[p], out_sem.at[3]).start()
+
+    steps = width // 256
     gather_near(full_i, 1, 2)
-
-    block = rd_r.at[pl.ds(0, 15)]
+    gather_rest(full_i, 1, 0)
+    gather_rest(full_i, 1, 1)
+    early(0, steps // 2)
+    gather_far(full_i, 1, 2)
+    early(steps // 2, steps)
+    block = ry_r.at[pl.ds(0, 15)]
     pltpu.make_async_copy(block, block, rt_r.at[1]).wait()
-    ro_s[...] = jnp.sum(rd_r[...], axis=0)
-    all_tensor(ro_s, ro_r, 2, True)
-    ro_r[t] = ro_s[...]
-    gather_far(full_i, 1, 2)
-    wait_tensor(ro_r, 2, rt_r)
-    for g in range(GROUPS):
-        part = slice(g * dgw, (g + 1) * dgw)
-        grad_router_ref[:8, part] = ro_r[g]
-        grad_router_ref[8:, part] = ro_r[4 + g]
-
-    for j in range(CHUNKS):
-        gather_rest(full_i, 1, j)
-
-    @pl.loop(0, width // 256)
-    def _(n):
-        at = pl.ds(pl.multiple_of(n * 256, 256), 256)
-        for src, dst, hbm, k in ((a_perm, gate, grad_gate_hbm, 2), (b_perm, up, grad_up_hbm, 3)):
-            total = None
-            for j in range(CHUNKS):
-                term = mm(src[j], full_i[j, :, :, at].reshape(rows, 256))
-                total = term if total is None else total + term
-            dst[at, :] = transposed(total.astype(BF16))
-            pltpu.make_async_copy(dst.at[at, :], hbm.at[at, :], out_sem.at[k]).start()
+    for k in range(16):
+        grad_router_ref[k : k + 1, :] = ry_r[k]
+    gather_rest(full_i, 1, 2)
+    for p in range(8):
+        late_in(p)
 
     down_out.wait()
     tokens_out.wait()
-    pltpu.make_async_copy(gate, grad_gate_hbm, out_sem.at[2]).wait()
-    pltpu.make_async_copy(up, grad_up_hbm, out_sem.at[3]).wait()
+    late_grad.wait()
+    pltpu.make_async_copy(weights, early_hbm, out_sem.at[2]).wait()
+    pltpu.make_async_copy(full_i.at[2], late_in_hbm, out_sem.at[3]).wait()
     for j in range(CHUNKS):
         a2a_drain(send_i, 1, j)
         a2a_drain(send_g, 2, j)
@@ -591,10 +573,68 @@
     pair_copy(CHUNKS - 1).wait_send()
     for n in range(4):
         rs_copy(CHUNKS - 1, n).wait_send()
-    wait_tensor(rp_s, 0, rt_s)
-    block = rd_r.at[pl.ds(0, 15)]
+    block = rx_r.at[pl.ds(0, 7)]
+    pltpu.make_async_copy(block, block, rt_s.at[0]).wait()
+    block = ry_r.at[pl.ds(0, 15)]
     pltpu.make_async_copy(block, block, rt_s.at[1]).wait()
-    wait_tensor(ro_r, 2, rt_s)
+
+
+def finish(
+    early_hbm,
+    late_in_hbm,
+    late_grad_hbm,
+    tokens_in,
+    down_in,
+    router_in,
+    gate_hbm,
+    up_hbm,
+    tokens_hbm,
+    down_hbm,
+    router_hbm,
+    early,
+    late_in,
+    late_grad,
+    tokens,
+    down,
+    router,
+    gate,
+    up,
+    in_sem,
+    out_sem,
+):
+    width, hidden = gate.shape
+    parts = 5
+    step = width // parts
+    stripes = [pl.ds(n * step, step) for n in range(parts)]
+    moves = [(late_grad_hbm, late_grad), (late_in_hbm, late_in)]
+    moves += [(early_hbm.at[at], early.at[at]) for at in stripes]
+    moves += [(down_in, down), (tokens_in, tokens), (router_in, router)]
+    loads = [pltpu.make_async_copy(a, b, in_sem.at[n]) for n, (a, b) in enumerate(moves)]
+    for load in loads:
+        load.start()
+    stores = []
+
+    def store(src, dst):
+        stores.append(pltpu.make_async_copy(src, dst, out_sem.at[len(stores)]))
+        stores[-1].start()
+
+    loads[0].wait()
+    loads[1].wait()
+    for n, at in enumerate(stripes):
+        loads[2 + n].wait()
+        value = mm(late_in[:, n * step : (n + 1) * step], late_grad[...], TN)
+        value = value + early[at, :].astype(F32)
+        gate[at, :] = value[:, :hidden].astype(BF16)
+        up[at, :] = value[:, hidden:].astype(BF16)
+        store(gate.at[at], gate_hbm.at[at])
+        store(up.at[at], up_hbm.at[at])
+    for n, (src, dst) in enumerate(
+        ((down, down_hbm), (tokens, tokens_hbm), (router, router_hbm))
+    ):
+        loads[2 + parts + n].wait()
+        store(src, dst)
+    for one in stores:
+        one.wait()
 
 
 def local(
@@ -622,26 +662,26 @@
         kernel,
         out_shape=(
             jax.ShapeDtypeStruct((count, width), BF16),
-            jax.ShapeDtypeStruct((width, hidden), BF16),
-            jax.ShapeDtypeStruct((width, hidden), BF16),
+            jax.ShapeDtypeStruct((width, 2 * hidden), BF16),
+            jax.ShapeDtypeStruct((8, 64, width), BF16),
+            jax.ShapeDtypeStruct((per, 2 * hidden), BF16),
             jax.ShapeDtypeStruct((hidden, width), BF16),
             jax.ShapeDtypeStruct((experts, width), F32),
         ),
         in_specs=[vmem] + [anywhere] * 8,
-        out_specs=(anywhere, anywhere, anywhere, anywhere, vmem),
+        out_specs=(anywhere, anywhere, anywhere, anywhere, anywhere, vmem),
         scratch_shapes=[
             pltpu.VMEM((count, width), BF16),
             pltpu.VMEM((count, width), BF16),
-            pltpu.VMEM((count, width), BF16),
-            pltpu.VMEM((width, experts), BF16),
-            pltpu.VMEM((width, hidden), BF16),
-            pltpu.VMEM((width, hidden), BF16),
+            pltpu.VMEM((CHUNKS, 64, width), BF16),
+            pltpu.VMEM((CHUNKS, 64, 128), F32),
+            pltpu.VMEM((experts, width), BF16),
+            pltpu.VMEM((width, 2 * hidden), BF16),
             pltpu.VMEM((hidden, width), BF16),
             pltpu.VMEM((CHUNKS, per, hidden), BF16),
             pltpu.VMEM((CHUNKS, per, hidden), BF16),
-            pltpu.VMEM((CHUNKS, hidden, per), BF16),
-            pltpu.VMEM((slots, hidden), BF16),
-            pltpu.VMEM((slots, hidden), BF16),
+            pltpu.VMEM((hidden, slots), BF16),
+            pltpu.VMEM((slots, 2 * hidden), BF16),
             folded,
             folded,
             folded,
@@ -659,16 +699,13 @@
             pltpu.VMEM((256, 256), BF16),
             pltpu.VMEM((256, 256), BF16),
             pltpu.VMEM((384, 384), BF16),
-            pltpu.VMEM((256, 256), BF16),
             pltpu.VMEM((count, width), F32),
             pltpu.VMEM((1, 128), jnp.int32),
             pltpu.VMEM((3, 128, 128), F32),
-            pltpu.VMEM((8, 8, dgw), F32),
-            pltpu.VMEM((8, 8, dgw), F32),
-            pltpu.VMEM((8, dgw), F32),
-            pltpu.VMEM((16, 8, dgw), F32),
-            pltpu.VMEM((8, dgw), F32),
-            pltpu.VMEM((8, 8, dgw), F32),
+            pltpu.VMEM((1, width), F32),
+            pltpu.VMEM((8, 1, width), F32),
+            pltpu.VMEM((1, width), F32),
+            pltpu.VMEM((16, 1, width), F32),
             dma((8,)),
             dma((3, CHUNKS)),
             dma((3, CHUNKS)),
@@ -678,9 +715,9 @@
             dma((CHUNKS,)),
             dma((CHUNKS, 4)),
             dma((CHUNKS, 4)),
-            dma((3,)),
-            dma((3,)),
-            dma((4,)),
+            dma((2,)),
+            dma((2,)),
+            dma((5,)),
         ],
         compiler_params=pltpu.CompilerParams(
             collective_id=0, has_side_effects=True, vmem_limit_bytes=63 * 2**20
@@ -694,14 +731,39 @@
         routing.reshape(1, count),
         tokens,
         out_grad,
-        router_weight,
+        router_weight.T,
         gate_weight[0],
         up_weight[0],
         down_weight[0],
         saved_gate[0],
         saved_up[0],
     )
-    grad_tokens, grad_gate, grad_up, grad_down, grad_router = outs
+    grad_tokens, early, late_in, late_grad, grad_down, grad_router = outs
+    grad_gate, grad_up, grad_tokens, grad_down, grad_router = pl.pallas_call(
+        finish,
+        out_shape=(
+            jax.ShapeDtypeStruct((width, hidden), BF16),
+            jax.ShapeDtypeStruct((width, hidden), BF16),
+            jax.ShapeDtypeStruct((count, width), BF16),
+            jax.ShapeDtypeStruct((hidden, width), BF16),
+            jax.ShapeDtypeStruct((experts, width), F32),
+        ),
+        in_specs=[anywhere] * 6,
+        out_specs=(anywhere,) * 5,
+        scratch_shapes=[
+            pltpu.VMEM((width, 2 * hidden), BF16),
+            pltpu.VMEM((per, width), BF16),
+            pltpu.VMEM((per, 2 * hidden), BF16),
+            pltpu.VMEM((count, width), BF16),
+            pltpu.VMEM((hidden, width), BF16),
+            pltpu.VMEM((experts, width), F32),
+            pltpu.VMEM((width, hidden), BF16),
+            pltpu.VMEM((width, hidden), BF16),
+            dma((10,)),
+            dma((13,)),
+        ],
+        compiler_params=pltpu.CompilerParams(vmem_limit_bytes=62 * 2**20),
+    )(early, late_in.reshape(per, width), late_grad, grad_tokens, grad_down, grad_router)
     return grad_tokens, grad_gate[None], grad_up[None], grad_down[None], grad_router.T
 
 

time: 163 us -> 137 us (0.84); the launches traced: 163 us -> 134 us
  Pallas kernels: 150 us -> 134 us
  local copies, waits for them, and re-layouts: 12.3 us -> 0 us
    pallas_call x1, Pallas kernels: 150 us -> 126 us  [local(): pl.pallas_call(kernel, out_shape=(jax.ShapeDtypeStruct((count, width), BF...]
    unnamed x12 -> x0, local copies, waits for them, and re-layouts: 12.3 us -> none
    pallas_call x0 -> x1, Pallas kernels: none -> 8.04 us  [local(): pl.pallas_call(finish, out_shape=(jax.ShapeDtypeStruct((width, hidden), B...]
where the time goes in v2:
time: 137 us; the launch traced here: 134 us
  Pallas kernels  134 us (98%)
    pallas_call x1, Pallas kernels, local(): pl.pallas_call(kernel, out_shape=(jax.ShapeDtypeStruct((count, width), BF...  126 us
    pallas_call x1, Pallas kernels, local(): pl.pallas_call(finish, out_shape=(jax.ShapeDtypeStruct((width, hidden), B...  8.04 us

profile of v2, /device:TPU:1, one launch (start us, length us, event | category | flops | bytes accessed | tf_op | source)
XLA Modules:
  0.0 134.4 jit_solution(9856763171218668325)
XLA Ops:
  0.6 125.5 %shard_map.128 = (bf16[128,2560]{1,0:T(8,128)(2,1)}, bf16[2560,1024]{1,0:T(8,128)(2,1)}, bf16[8,64,2560]{2,1,0:T(8,128)(2,1)}, bf16[512,1024]{1,0:T(8,128)(2,1)}...) custom-call(s32[1,128]{1,0:T(1,128)} %bitcast.23, bf16[128,2560]{1,0:T(8,128)(2,1)} %tokens_hbm.1, ...), custom_call_target="tpu_custom_call" | custom-call | flops 24159191040 | bytes 21495808 | tf_op jit(solution)/shard_map/pallas_call | solution.py:661
  126.2 8.0 %shard_map.129 = (bf16[2560,512]{1,0:T(8,128)(2,1)}, bf16[2560,512]{1,0:T(8,128)(2,1)}, bf16[128,2560]{1,0:T(8,128)(2,1)}, bf16[512,2560]{1,0:T(8,128)(2,1)}, f32[16,2560]{1,0:T(8,128)}) custom-call(bf16[2560,1024]{1,0:T(8,128)(2,1)} %get-tuple-element.16.early_hbm, bf16[512,2560]{1,0:T(8,128)(2,1)} %bitcast.12, ...), custom_call_target="tpu_custom_call" | custom-call | tf_op jit(solution)/shard_map/pallas_call | solution.py:742

commit v3 on v2

--- a/solution.py
+++ b/solution.py
@@ -14,6 +14,7 @@
 
 CHUNKS = 3
 GROUPS = 4
+CROSSED = 1
 
 
 def mm(a, b, dims=NN):
@@ -73,6 +74,9 @@
     fold_m,
     save_m,
     gs,
+    crossed,
+    send_a,
+    recv_a,
     tgt_row,
     cols,
     rx_s,
@@ -82,6 +86,10 @@
     load_sem,
     a2a_s,
     a2a_r,
+    cr_s,
+    cr_r,
+    ca_s,
+    ca_r,
     ag_s,
     ag_r,
     pc_s,
@@ -107,6 +115,7 @@
     rows = full_g.shape[1] * full_g.shape[2]
     width = tok.shape[1]
     hidden = down.shape[0]
+    cut = CROSSED * dgw
 
     loads = [
         pltpu.make_async_copy(src, dst, load_sem.at[n])
@@ -168,16 +177,21 @@
         part = src.at[j, pl.ds(0, 15)]
         pltpu.make_async_copy(part, part, a2a_s.at[kind, j]).wait()
 
+    def piece(buf, kind, j, p, first=0, count=64):
+        if kind == 0:
+            return buf.at[j, p, pl.ds(first, count)]
+        return buf.at[j, p, pl.ds(first, count), pl.ds(cut, width - cut)]
+
     def gather_copy(buf, kind, j, n):
         block, to = (
-            (buf.at[j, mine], right),
-            (buf.at[j, mine], left),
-            (buf.at[j, from_left, pl.ds(0, 32)], right),
-            (buf.at[j, from_right, pl.ds(32, 32)], left),
-            (buf.at[j, mine], partner),
-            (buf.at[j, from_left], partner),
-            (buf.at[j, from_right], partner),
-            (buf.at[j, far], partner),
+            (piece(buf, kind, j, mine), right),
+            (piece(buf, kind, j, mine), left),
+            (piece(buf, kind, j, from_left, 0, 32), right),
+            (piece(buf, kind, j, from_right, 32, 32), left),
+            (piece(buf, kind, j, mine), partner),
+            (piece(buf, kind, j, from_left), partner),
+            (piece(buf, kind, j, from_right), partner),
+            (piece(buf, kind, j, far), partner),
         )[n]
         return remote(block, block, ag_s.at[kind, j, n], ag_r.at[kind, j, n], to)
 
@@ -188,14 +202,14 @@
     def landed(buf, kind, j, n):
         other = (1 - c) * 4
         block = (
-            lambda: buf.at[j, from_left],
-            lambda: buf.at[j, from_right],
-            lambda: buf.at[j, far, pl.ds(0, 32)],
-            lambda: buf.at[j, far, pl.ds(32, 32)],
-            lambda: buf.at[j, other + y],
-            lambda: buf.at[j, other + lax.rem(y + 3, 4)],
-            lambda: buf.at[j, other + lax.rem(y + 1, 4)],
-            lambda: buf.at[j, other + lax.rem(y + 2, 4)],
+            lambda: piece(buf, kind, j, from_left),
+            lambda: piece(buf, kind, j, from_right),
+            lambda: piece(buf, kind, j, far, 0, 32),
+            lambda: piece(buf, kind, j, far, 32, 32),
+            lambda: piece(buf, kind, j, other + y),
+            lambda: piece(buf, kind, j, other + lax.rem(y + 3, 4)),
+            lambda: piece(buf, kind, j, other + lax.rem(y + 1, 4)),
+            lambda: piece(buf, kind, j, other + lax.rem(y + 2, 4)),
         )[n]()
         remote(block, block, ag_s.at[kind, j, n], ag_r.at[kind, j, n], partner).wait_recv()
 
@@ -225,7 +239,7 @@
     high = (slot >= 4.0).astype(F32) + (slot >= 8.0).astype(F32)
     e_float = e_row.astype(F32)
     target = high * 252.0 + e_float * 16.0 + slot
-    tgt_row[...] = target.astype(jnp.int32)
+    tgt_row[y] = target.astype(jnp.int32)
     eye128 = eye_mask(128)
 
     def to_column(row):
@@ -240,10 +254,74 @@
     def fold_tokens(src, dst, j):
         total = None
         for g in range(GROUPS):
-            place = (iota((256, 128), 0) == tgt_row[...] + (4 * g - 256 * j)).astype(BF16)
+            place = (iota((256, 128), 0) == tgt_row[y] + (4 * g - 256 * j)).astype(BF16)
             term = mm(place, src[:, g * dgw : (g + 1) * dgw])
             total = term if total is None else total + term
         dst[j] = total.astype(BF16).reshape(16, 16, dgw)
+
+    crossing = (
+        (crossed.at[y], right),
+        (crossed.at[y], left),
+        (crossed.at[lax.rem(y + 3, 4), pl.ds(0, 64)], right),
+        (crossed.at[lax.rem(y + 1, 4), pl.ds(64, 64)], left),
+    )
+
+    def cross_copy(n):
+        block, to = crossing[n]
+        return remote(block, block, cr_s.at[n], cr_r.at[n], to)
+
+    def target_copy(k):
+        to = (d, lax.rem(y + k, 4) * 2 + c)
+        return remote(tgt_row.at[y], tgt_row.at[y], cr_s.at[4 + k], cr_r.at[4 + k], to)
+
+    def cross_landed(n):
+        block = (
+            crossed.at[lax.rem(y + 3, 4)],
+            crossed.at[lax.rem(y + 1, 4)],
+            crossed.at[lax.rem(y + 2, 4), pl.ds(0, 64)],
+            crossed.at[lax.rem(y + 2, 4), pl.ds(64, 64)],
+        )[n]
+        remote(block, block, cr_s.at[n], cr_r.at[n], right).wait_recv()
+
+    def cross_own():
+        for k in (1, 2, 3):
+            target_copy(k).start()
+        cross_copy(0).start()
+        cross_copy(1).start()
+
+    def cross_near():
+        cross_landed(0)
+        cross_copy(2).start()
+        cross_landed(1)
+        cross_copy(3).start()
+
+    def cross_far():
+        for k in (1, 2, 3):
+            block = tgt_row.at[lax.rem(y + 4 - k, 4)]
+            remote(block, block, cr_s.at[4 + k], cr_r.at[4 + k], right).wait_recv()
+        cross_landed(2)
+        cross_landed(3)
+
+    def cross_send(j):
+        for g in range(CROSSED):
+            total = None
+            for p in range(4):
+                place = (iota((256, 128), 0) == tgt_row[p] + (4 * p - 256 * j)).astype(BF16)
+                term = mm(place, crossed[p, :, g * dgw : (g + 1) * dgw])
+                total = term if total is None else total + term
+            send_a[g, j] = total.astype(BF16).reshape(16, 16, dgw)
+            a2a_start(send_a.at[g], recv_a.at[g], 3 + g, j)
+
+    def cross_pair(j, parity):
+        block = full_i.at[j, pl.ds(parity * 4, 4), :, pl.ds(0, cut)]
+        return remote(block, block, ca_s.at[j], ca_r.at[j], partner)
+
+    def cross_take(j):
+        for g in range(CROSSED):
+            a2a_wait(recv_a.at[g], 3 + g, j)
+            moved = mm(unfold_m[...], recv_a[g, j].reshape(256, dgw)).astype(BF16)
+            full_i[j, pl.ds(c * 4, 4), :, g * dgw : (g + 1) * dgw] = moved.reshape(4, 64, dgw)
+        cross_pair(j, c).start()
 
     out_at = iota((256, 256), 0)
     in_at = iota((256, 256), 1)
@@ -403,7 +481,7 @@
         logit = jnp.sum(jnp.where(iota((64, 16), 1) == d, logits, 0.0), axis=1, keepdims=True)
         score = jax.nn.sigmoid(logit)
         row_score[j] = jnp.broadcast_to(score, (64, 128))
-        full_i[j, mine] = (score * tok_rows[j].astype(F32)).astype(BF16)
+        full_i[j, mine, :, cut:] = (score * tok_rows[j, :, cut:].astype(F32)).astype(BF16)
 
     loads[0].wait()
     for j in range(CHUNKS):
@@ -414,29 +492,45 @@
     for load in loads[3:]:
         load.start()
     loads[1].wait()
-    for j in range(CHUNKS):
-        own_grads(j)
+    loads[2].wait()
+    logits = mm(tok[...], rw[...], NT)
+    lane_e = iota((128, 16), 1).astype(F32)
+    onehot = (lane_e == cols[1][:, :16]).astype(F32)
+    score = jax.nn.sigmoid(jnp.sum(logits * onehot, axis=1, keepdims=True))
+    cols[2] = jnp.broadcast_to(score, (128, 128))
+    crossed[y] = (score * tok[:, :cut].astype(F32)).astype(BF16)
+    cross_own()
+    own_grads(0)
+    own_grads(1)
+    fold_tokens(tok, send_i, 0)
+    a2a_start(send_i, recv_i, 1, 0)
+    cross_near()
+    own_grads(2)
+    gather_near(full_g, 0, 0)
+    for j in (1, 2):
         fold_tokens(tok, send_i, j)
         a2a_start(send_i, recv_i, 1, j)
-    gather_near(full_g, 0, 0)
     loads[3].wait()
     loads[4].wait()
     permute_saved(0, a_perm)
     gather_near(full_g, 0, 1)
     permute_saved(hidden, b_perm)
+    cross_far()
+    cross_send(0)
     gather_far(full_g, 0, 0)
     for load in loads[5:]:
         load.wait()
-    loads[2].wait()
     own_inputs(0)
     gather_near(full_g, 0, 2)
     gather_own(full_i, 1, 0)
+    cross_send(1)
     gather_rest(full_g, 0, 0)
     compute(0)
     gather_far(full_g, 0, 1)
     partials(0)
     gather_far(full_g, 0, 2)
     reduce_far(0)
+    cross_send(2)
     gather_rest(full_g, 0, 1)
     compute(1)
     partials(1)
@@ -451,6 +545,7 @@
     own_inputs(1)
     gather_own(full_i, 1, 1)
     reduce_last(0)
+    cross_take(0)
     own_inputs(2)
     late_grad = pltpu.make_async_copy(
         gab.at[pl.ds(2 * rows, rows)], late_grad_hbm, out_sem.at[4]
@@ -459,13 +554,10 @@
     make_hidden(0)
     make_hidden(1)
     make_hidden(2)
-    logits = mm(tok[...], rw[...], NT)
-    lane_e = iota((128, 16), 1).astype(F32)
-    onehot = (lane_e == cols[1][:, :16]).astype(F32)
-    score = jax.nn.sigmoid(jnp.sum(logits * onehot, axis=1, keepdims=True))
-    cols[2] = jnp.broadcast_to(score, (128, 128))
     reduce_near(2)
     gather_far(full_i, 1, 0)
+    cross_take(1)
+    cross_take(2)
 
     tile = 512
 
@@ -503,8 +595,9 @@
 
     bring_back(0)
     bring_back(1)
+    bring_back(2)
     gather_far(full_i, 1, 1)
-    bring_back(2)
+    gather_near(full_i, 1, 2)
     score = cols[2][:, :1]
     grad_score = jnp.zeros((128, 1), F32)
     for g in range(GROUPS):
@@ -545,19 +638,27 @@
         pltpu.make_async_copy(full_i.at[2, p], late_in_hbm.at[p], out_sem.at[3]).start()
 
     steps = width // 256
-    gather_near(full_i, 1, 2)
-    gather_rest(full_i, 1, 0)
-    gather_rest(full_i, 1, 1)
+    for j in (0, 1):
+        gather_rest(full_i, 1, j)
+        cross_pair(j, 1 - c).wait_recv()
     early(0, steps // 2)
     gather_far(full_i, 1, 2)
     early(steps // 2, steps)
+    cross_pair(2, 1 - c).wait_recv()
+    for n in (4, 5, 6):
+        landed(full_i, 1, 2, n)
+    other = (1 - c) * 4
+    late_in(other + y)
+    late_in(other + lax.rem(y + 1, 4))
+    late_in(other + lax.rem(y + 3, 4))
+    for p in range(4):
+        late_in(c * 4 + p)
     block = ry_r.at[pl.ds(0, 15)]
     pltpu.make_async_copy(block, block, rt_r.at[1]).wait()
     for k in range(16):
         grad_router_ref[k : k + 1, :] = ry_r[k]
-    gather_rest(full_i, 1, 2)
-    for p in range(8):
-        late_in(p)
+    landed(full_i, 1, 2, 7)
+    late_in(other + lax.rem(y + 2, 4))
 
     down_out.wait()
     tokens_out.wait()
@@ -570,6 +671,14 @@
         for n in range(8):
             gather_copy(full_g, 0, j, n).wait_send()
             gather_copy(full_i, 1, j, n).wait_send()
+    for n in range(4):
+        cross_copy(n).wait_send()
+    for k in (1, 2, 3):
+        target_copy(k).wait_send()
+    for j in range(CHUNKS):
+        cross_pair(j, c).wait_send()
+        for g in range(CROSSED):
+            a2a_drain(send_a.at[g], 3 + g, j)
     pair_copy(CHUNKS - 1).wait_send()
     for n in range(4):
         rs_copy(CHUNKS - 1, n).wait_send()
@@ -700,15 +809,22 @@
             pltpu.VMEM((256, 256), BF16),
             pltpu.VMEM((384, 384), BF16),
             pltpu.VMEM((count, width), F32),
-            pltpu.VMEM((1, 128), jnp.int32),
+            pltpu.VMEM((4, count, CROSSED * dgw), BF16),
+            pltpu.VMEM((CROSSED, CHUNKS, experts, 16, dgw), BF16),
+            pltpu.VMEM((CROSSED, CHUNKS, experts, 16, dgw), BF16),
+            pltpu.VMEM((4, 1, 128), jnp.int32),
             pltpu.VMEM((3, 128, 128), F32),
             pltpu.VMEM((1, width), F32),
             pltpu.VMEM((8, 1, width), F32),
             pltpu.VMEM((1, width), F32),
             pltpu.VMEM((16, 1, width), F32),
             dma((8,)),
-            dma((3, CHUNKS)),
-            dma((3, CHUNKS)),
+            dma((3 + CROSSED, CHUNKS)),
+            dma((3 + CROSSED, CHUNKS)),
+            dma((8,)),
+            dma((8,)),
+            dma((CHUNKS,)),
+            dma((CHUNKS,)),
             dma((2, CHUNKS, 8)),
             dma((2, CHUNKS, 8)),
             dma((CHUNKS,)),

time: 137 us -> 133 us (0.971); the launches traced: 134 us -> 132 us
  Pallas kernels: 134 us -> 131 us
    pallas_call x1, Pallas kernels: 126 us -> 123 us  [local(): pl.pallas_call(kernel, out_shape=(jax.ShapeDtypeStruct((count, width), BF...]
where the time goes in v3:
time: 133 us; the launch traced here: 132 us
  Pallas kernels  131 us (98%)
    pallas_call x1, Pallas kernels, local(): pl.pallas_call(kernel, out_shape=(jax.ShapeDtypeStruct((count, width), BF...  123 us
    pallas_call x1, Pallas kernels, local(): pl.pallas_call(finish, out_shape=(jax.ShapeDtypeStruct((width, hidden), B...  8.05 us

profile of v3, /device:TPU:1, one launch (start us, length us, event | category | flops | bytes accessed | tf_op | source)
XLA Modules:
  0.0 131.7 jit_solution(14447778659433748781)
XLA Ops:
  0.6 122.9 %shard_map.128 = (bf16[128,2560]{1,0:T(8,128)(2,1)}, bf16[2560,1024]{1,0:T(8,128)(2,1)}, bf16[8,64,2560]{2,1,0:T(8,128)(2,1)}, bf16[512,1024]{1,0:T(8,128)(2,1)}...) custom-call(s32[1,128]{1,0:T(1,128)} %bitcast.23, bf16[128,2560]{1,0:T(8,128)(2,1)} %tokens_hbm.1, ...), custom_call_target="tpu_custom_call" | custom-call | flops 24159191040 | bytes 21495808 | tf_op jit(solution)/shard_map/pallas_call | solution.py:770
  123.5 8.1 %shard_map.129 = (bf16[2560,512]{1,0:T(8,128)(2,1)}, bf16[2560,512]{1,0:T(8,128)(2,1)}, bf16[128,2560]{1,0:T(8,128)(2,1)}, bf16[512,2560]{1,0:T(8,128)(2,1)}, f32[16,2560]{1,0:T(8,128)}) custom-call(bf16[2560,1024]{1,0:T(8,128)(2,1)} %get-tuple-element.16.early_hbm, bf16[512,2560]{1,0:T(8,128)(2,1)} %bitcast.12, ...), custom_call_target="tpu_custom_call" | custom-call | tf_op jit(solution)/shard_map/pallas_call | solution.py:858

commit v4 on v3

--- a/solution.py
+++ b/solution.py
@@ -528,19 +528,19 @@
     compute(0)
     gather_far(full_g, 0, 1)
     partials(0)
+    reduce_far(0)
     gather_far(full_g, 0, 2)
-    reduce_far(0)
     cross_send(2)
     gather_rest(full_g, 0, 1)
     compute(1)
+    reduce_near(0)
     partials(1)
-    reduce_near(0)
     reduce_far(1)
     gather_rest(full_g, 0, 2)
     compute(2)
     gather_near(full_i, 1, 0)
+    reduce_near(1)
     partials(2)
-    reduce_near(1)
     reduce_far(2)
     own_inputs(1)
     gather_own(full_i, 1, 1)
@@ -558,7 +558,6 @@
     gather_far(full_i, 1, 0)
     cross_take(1)
     cross_take(2)
-
     tile = 512
 
     @pl.loop(0, width // tile)
@@ -572,7 +571,6 @@
     gather_near(full_i, 1, 1)
     gather_own(full_i, 1, 2)
     reduce_last(2)
-
     @pl.loop(1, 8)
     def _(k):
         to = lax.rem(t + k, 8)
@@ -593,6 +591,20 @@
             else:
                 gs[:, part] += moved
 
+    def early(first, last):
+        @pl.loop(first, last)
+        def _(n):
+            at = pl.ds(pl.multiple_of(n * 256, 256), 256)
+            value = mm(full_i[:2, :, :, at].reshape(2 * rows, 256), gab[: 2 * rows, :], TN)
+            weights[at, :] = value.astype(BF16)
+            pltpu.make_async_copy(
+                weights.at[at, :], early_hbm.at[at, :], out_sem.at[2]
+            ).start()
+
+    def late_in(p):
+        pltpu.make_async_copy(full_i.at[2, p], late_in_hbm.at[p], out_sem.at[3]).start()
+
+    steps = width // 256
     bring_back(0)
     bring_back(1)
     bring_back(2)
@@ -624,23 +636,10 @@
 
     ry_r[d] = ry_s[...]
 
-    def early(first, last):
-        @pl.loop(first, last)
-        def _(n):
-            at = pl.ds(pl.multiple_of(n * 256, 256), 256)
-            value = mm(full_i[:2, :, :, at].reshape(2 * rows, 256), gab[: 2 * rows, :], TN)
-            weights[at, :] = value.astype(BF16)
-            pltpu.make_async_copy(
-                weights.at[at, :], early_hbm.at[at, :], out_sem.at[2]
-            ).start()
-
-    def late_in(p):
-        pltpu.make_async_copy(full_i.at[2, p], late_in_hbm.at[p], out_sem.at[3]).start()
-
-    steps = width // 256
-    for j in (0, 1):
-        gather_rest(full_i, 1, j)
-        cross_pair(j, 1 - c).wait_recv()
+    gather_rest(full_i, 1, 0)
+    cross_pair(0, 1 - c).wait_recv()
+    gather_rest(full_i, 1, 1)
+    cross_pair(1, 1 - c).wait_recv()
     early(0, steps // 2)
     gather_far(full_i, 1, 2)
     early(steps // 2, steps)

time: 133 us -> 130 us (0.977)
  Pallas kernels: 131 us -> 129 us
    pallas_call x1, Pallas kernels: 123 us -> 121 us  [local(): pl.pallas_call(kernel, out_shape=(jax.ShapeDtypeStruct((count, width), BF...]
where the time goes in v4:
time: 130 us
  Pallas kernels  129 us (99%)
    pallas_call x1, Pallas kernels, local(): pl.pallas_call(kernel, out_shape=(jax.ShapeDtypeStruct((count, width), BF...  121 us
    pallas_call x1, Pallas kernels, local(): pl.pallas_call(finish, out_shape=(jax.ShapeDtypeStruct((width, hidden), B...  8.05 us

profile of v4, /device:TPU:1, one launch (start us, length us, event | category | flops | bytes accessed | tf_op | source)
XLA Modules:
  0.0 129.7 jit_solution(7539303163775399331)
XLA Ops:
  0.6 120.9 %shard_map.128 = (bf16[128,2560]{1,0:T(8,128)(2,1)}, bf16[2560,1024]{1,0:T(8,128)(2,1)}, bf16[8,64,2560]{2,1,0:T(8,128)(2,1)}, bf16[512,1024]{1,0:T(8,128)(2,1)}...) custom-call(s32[1,128]{1,0:T(1,128)} %bitcast.23, bf16[128,2560]{1,0:T(8,128)(2,1)} %tokens_hbm.1, ...), custom_call_target="tpu_custom_call" | custom-call | flops 24159191040 | bytes 21495808 | tf_op jit(solution)/shard_map/pallas_call | solution.py:769
  121.5 8.0 %shard_map.129 = (bf16[2560,512]{1,0:T(8,128)(2,1)}, bf16[2560,512]{1,0:T(8,128)(2,1)}, bf16[128,2560]{1,0:T(8,128)(2,1)}, bf16[512,2560]{1,0:T(8,128)(2,1)}, f32[16,2560]{1,0:T(8,128)}) custom-call(bf16[2560,1024]{1,0:T(8,128)(2,1)} %get-tuple-element.16.early_hbm, bf16[512,2560]{1,0:T(8,128)(2,1)} %bitcast.12, ...), custom_call_target="tpu_custom_call" | custom-call | tf_op jit(solution)/shard_map/pallas_call | solution.py:857
